TPU v7x, 32 devices: a whole 2x2x4 slice. The times are simulated.
32 devices in a mesh: frames: 16 (over z, y, x), dp: 2 (over core).
Axes of the slice: x: 2, y: 2, z: 4, core: 2. Of those that a mesh axis runs over, the one named last changes fastest.
Arguments:
- latents: bfloat16 [2, 16, 1024, 4], P('dp', 'frames'), may hold values from -6 to 6
- noise: bfloat16 [2, 16, 1024, 4], P('dp', 'frames'), may hold values from -6 to 6
- timesteps: int32 [2, 1], P('dp'), may hold values from 0 to 999
- image_flags: int32 [2, 1], P('dp'), may hold values 0 or 1
- frame_counts: int32 [2, 1], replicated, may hold values from 1 to 16, as said below
- text: bfloat16 [2, 1, 77, 768], P('dp'), may hold values from -6 to 6
- conv_in: bfloat16 [3, 3, 4, 320], replicated, may hold values from -1 to 1
- res_convs: bfloat16 [2, 3, 3, 320, 320], replicated, may hold values from -0.109375 to 0.109375
- conv_out: bfloat16 [3, 3, 320, 4], replicated, may hold values from -0.109375 to 0.109375
- time_w1: bfloat16 [320, 1280], replicated, may hold values from -0.3125 to 0.3125
- time_w2: bfloat16 [1280, 1280], replicated, may hold values from -0.15625 to 0.15625
- temb_w: bfloat16 [1280, 320], replicated, may hold values from -0.15625 to 0.15625
- spatial_squares: bfloat16 [8, 320, 320], replicated, may hold values from -0.3125 to 0.3125
- cross_kv: bfloat16 [768, 640], replicated, may hold values from -0.21875 to 0.21875
- spatial_up: bfloat16 [320, 2560], replicated, may hold values from -0.3125 to 0.3125
- spatial_down: bfloat16 [1280, 320], replicated, may hold values from -0.15625 to 0.15625
- frozen_vectors: float32 [23, 320], replicated
- motion_squares: float32 [10, 320, 320], replicated, may hold values from -0.3125 to 0.3125
- motion_up: float32 [320, 2560], replicated, may hold values from -0.3125 to 0.3125
- motion_down: float32 [1280, 320], replicated, may hold values from -0.15625 to 0.15625
- motion_vectors: float32 [13, 320], replicated
- square_moment: float32 [10, 320, 320], P('dp'), may hold values from -0.0048828125 to 0.0048828125
- up_moment: float32 [320, 2560], P(None, 'dp'), may hold values from -0.0048828125 to 0.0048828125
- down_moment: float32 [1280, 320], P('dp'), may hold values from -0.0048828125 to 0.0048828125
- vector_moment1: float32 [13, 320], replicated, may hold values from -0.00048828125 to 0.00048828125
- vector_moment2: float32 [13, 320], replicated, may hold values from 1.0986328e-10 to 4.394531e-10
- square_ema: float32 [10, 320, 320], P('dp'), may hold values from -0.3125 to 0.3125
- up_ema: float32 [320, 2560], P(None, 'dp'), may hold values from -0.3125 to 0.3125
- down_ema: float32 [1280, 320], P('dp'), may hold values from -0.15625 to 0.15625
- vector_ema: float32 [13, 320], replicated, may hold values from 0.5 to 1.5
Outputs:
- loss_sum: float32 [], replicated
- frame_total: float32 [], replicated
- square_weights_new: float32 [10, 320, 320], replicated
- square_moment_new: float32 [10, 320, 320], P('dp')
- square_ema_new: float32 [10, 320, 320], P('dp')
- up_weights_new: float32 [320, 2560], replicated
- up_moment_new: float32 [320, 2560], P(None, 'dp')
- up_ema_new: float32 [320, 2560], P(None, 'dp')
- down_weights_new: float32 [1280, 320], replicated
- down_moment_new: float32 [1280, 320], P('dp')
- down_ema_new: float32 [1280, 320], P('dp')
- vector_moment1_new: float32 [13, 320], replicated
- vector_moment2_new: float32 [13, 320], replicated
- vector_weights_new: float32 [13, 320], replicated
- vector_ema_new: float32 [13, 320], replicated
Inputs may be any that keep to these rules, and one draw needn't show every extreme that they name: `frame_counts`: the first that many of a sample's 16 frames are valid; in each group one sample has all 16 frames valid.
All inputs are finite; a program needn't handle non-finite values. No bound on the sum of `image_flags` on one device may be relied on, other than what follows from the above.
Results may differ from a plain program's by a relative error of at most 0.0094.
Values may be sent and summed in bfloat16 or wider, within the bound.
No kernel may reach another device: no remote copies, remote signals or barrier semaphores. Data moves between devices by JAX's collectives and lax.ppermute only.
A program may use at most 256 MiB of HBM per device.

v0:
```python
import math

import jax
import jax.numpy as jnp
from jax import lax
from jax.sharding import PartitionSpec as P

WIDTH = 320
HEADS = 8
HEAD_DIM = 40
FF_INNER = 1280
TEXT_LEN = 77
TEXT_DIM = 768
GN_GROUPS = 32
CLIP = 16
LATENT = 32
STEP = 10
PIX = 1024


PRECISE = lax.Precision.HIGHEST
MUON_RATE = 0.2
ADAM_RATE = 0.4
DECAY = 0.01
AVERAGE = 0.75


def to_low(values):
    return values.astype(jnp.bfloat16)


def product(left, right):
    return jnp.einsum("...i,ij->...j", left, right, preferred_element_type=jnp.float32)


def product_back(left, right):
    return jnp.einsum("...j,ij->...i", left, right, preferred_element_type=jnp.float32)


def convolve(values, kernel):
    leading = values.shape[:-2]
    images = values.reshape((-1, LATENT, LATENT, values.shape[-1]))
    result = lax.conv_general_dilated(
        images,
        kernel,
        (1, 1),
        "SAME",
        dimension_numbers=("NHWC", "HWIO", "NHWC"),
        preferred_element_type=jnp.float32,
    )
    return result.reshape(leading + (PIX, kernel.shape[-1]))


def group_norm(values, scaling, offset):
    full_shape = values.shape
    grouped = values.reshape(full_shape[:-1] + (GN_GROUPS, full_shape[-1] // GN_GROUPS))
    centre = jnp.mean(grouped, axis=(-3, -1), keepdims=True)
    spread = jnp.mean(jnp.square(grouped - centre), axis=(-3, -1), keepdims=True)
    return ((grouped - centre) * lax.rsqrt(spread + 1e-05)).reshape(full_shape) * scaling + offset


def layer_norm(values, scaling, offset):
    centre = jnp.mean(values, axis=-1, keepdims=True)
    spread = jnp.mean(jnp.square(values - centre), axis=-1, keepdims=True)
    return (values - centre) * lax.rsqrt(spread + 1e-05) * scaling + offset


def gated_gelu(gate_up):
    return gate_up[..., :FF_INNER] * jax.nn.gelu(gate_up[..., FF_INNER:], approximate=False)


def frame_codes():
    positions = jnp.arange(CLIP, dtype=jnp.float32)[:, None]
    column = jnp.arange(WIDTH)
    frequency = jnp.exp(-math.log(10000.0) * (2 * (column // 2)).astype(jnp.float32) / WIDTH)
    angles = positions * frequency
    return jnp.where(column % 2 == 0, jnp.sin(angles), jnp.cos(angles))


def spatial_attend(queries, key_vecs, values):
    query_heads = queries.reshape(queries.shape[0], HEADS, HEAD_DIM)
    key_heads = key_vecs.reshape(key_vecs.shape[0], HEADS, HEAD_DIM)
    value_heads = values.reshape(values.shape[0], HEADS, HEAD_DIM)
    scores = jnp.einsum(
        "qhd,khd->hqk", query_heads, key_heads, preferred_element_type=jnp.float32
    ) / math.sqrt(HEAD_DIM)
    probs_low = to_low(jax.nn.softmax(scores, axis=-1))
    mixture = jnp.einsum("hqk,khd->qhd", probs_low, value_heads, preferred_element_type=jnp.float32)
    return to_low(mixture.reshape(queries.shape[0], WIDTH))


def time_embed(step_values, time_w1, time_w2, temb_w, temb_bias):
    half_width = WIDTH // 2
    frequency = jnp.exp(-math.log(10000.0) * jnp.arange(half_width, dtype=jnp.float32) / half_width)
    angles = step_values[..., None] * frequency
    encoding = jnp.concatenate([jnp.cos(angles), jnp.sin(angles)], axis=-1)
    hidden = product(to_low(encoding), time_w1)
    hidden = product(to_low(jax.nn.silu(hidden)), time_w2)
    return product(to_low(jax.nn.silu(hidden)), temb_w) + temb_bias


def frame_forward(noisy_frame, temb_row, text_rows, frozen):
    conv_in, res_convs, squares, cross_kv, spatial_up, spatial_down, vectors = frozen
    first_conv = convolve(to_low(noisy_frame), conv_in) + vectors[0]
    inner_act = (
        convolve(to_low(jax.nn.silu(group_norm(first_conv, vectors[1], vectors[2]))), res_convs[0])
        + vectors[3]
        + temb_row
    )
    inner_act = (
        convolve(to_low(jax.nn.silu(group_norm(inner_act, vectors[4], vectors[5]))), res_convs[1])
        + vectors[6]
    )
    resnet = first_conv + inner_act
    tokens = product(to_low(group_norm(resnet, vectors[7], vectors[8])), squares[0]) + vectors[9]
    normal_a = to_low(layer_norm(tokens, vectors[10], vectors[11]))
    mixture = spatial_attend(
        to_low(product(normal_a, squares[1])),
        to_low(product(normal_a, squares[2])),
        to_low(product(normal_a, squares[3])),
    )
    tokens = tokens + (product(mixture, squares[4]) + vectors[12])
    normal_c = to_low(layer_norm(tokens, vectors[13], vectors[14]))
    text_kv = to_low(product(text_rows, cross_kv))
    mixture = spatial_attend(
        to_low(product(normal_c, squares[5])), text_kv[:, :WIDTH], text_kv[:, WIDTH:]
    )
    tokens = tokens + (product(mixture, squares[6]) + vectors[15])
    normal_f = to_low(layer_norm(tokens, vectors[16], vectors[17]))
    tokens = tokens + (
        product(to_low(gated_gelu(product(normal_f, spatial_up))), spatial_down) + vectors[18]
    )
    return resnet + (product(to_low(tokens), squares[7]) + vectors[19])


def temporal_forward(stream, squares, first, gain, offset, masking):
    normal_a = to_low(layer_norm(stream, gain, offset) + frame_codes())
    queries = to_low(product(normal_a, squares[first]))
    key_vecs = to_low(product(normal_a, squares[first + 1]))
    values = to_low(product(normal_a, squares[first + 2]))
    head_shape = queries.shape[:-1] + (HEADS, HEAD_DIM)
    scores = (
        jnp.einsum(
            "psfhd,psehd->pshfe",
            queries.reshape(head_shape),
            key_vecs.reshape(head_shape),
            preferred_element_type=jnp.float32,
        )
        / math.sqrt(HEAD_DIM)
        + masking[None, :, None, None, :]
    )
    softmaxed = jax.nn.softmax(scores, axis=-1)
    probs_low = to_low(softmaxed)
    mixture = to_low(
        jnp.einsum(
            "pshfe,psehd->psfhd",
            probs_low,
            values.reshape(head_shape),
            preferred_element_type=jnp.float32,
        ).reshape(queries.shape)
    )
    return (mixture, (normal_a, queries, key_vecs, values, softmaxed, probs_low, mixture))


def motion_forward(arrived, masking, keep_video, low_weights, vectors):
    squares, up_weight, down_weight = low_weights
    inputs = to_low(arrived.astype(jnp.float32) * vectors[0] + vectors[1])
    motion_u = product(inputs, squares[0]) + vectors[2]
    mixture, kept_first = temporal_forward(motion_u, squares, 1, vectors[3], vectors[4], masking)
    middle = motion_u + (product(mixture, squares[4]) + vectors[5])
    mixture, kept_second = temporal_forward(middle, squares, 5, vectors[6], vectors[7], masking)
    upper = middle + (product(mixture, squares[8]) + vectors[8])
    normal_c = to_low(layer_norm(upper, vectors[9], vectors[10]))
    gate_up = product(normal_c, up_weight)
    inner_act = to_low(gated_gelu(gate_up))
    final_u = upper + (product(inner_act, down_weight) + vectors[11])
    final_low = to_low(final_u)
    branch = to_low((product(final_low, squares[9]) + vectors[12]) * keep_video)
    saved = (
        inputs,
        motion_u,
        kept_first,
        middle,
        kept_second,
        upper,
        normal_c,
        gate_up,
        inner_act,
        final_low,
    )
    return (branch, saved)


def contract(left, right):
    return jnp.einsum("psfi,psfj->ij", left, right, preferred_element_type=jnp.float32)


def column_sum(values):
    return jnp.sum(values.astype(jnp.float32), axis=(0, 1, 2))


def temporal_backward(grad_stream, stream, squares, first, gain, offset, kept):
    normal_a, queries, key_vecs, values, softmaxed, probs_low, mixture = kept
    head_shape = queries.shape[:-1] + (HEADS, HEAD_DIM)
    grad_attn = to_low(grad_stream)
    w_o_grad = contract(mixture, grad_attn)
    b_o_grad = column_sum(grad_attn)
    grad_mixture = to_low(product_back(grad_attn, squares[first + 3])).reshape(head_shape)
    grad_values = jnp.einsum(
        "pshfe,psfhd->psehd", probs_low, grad_mixture, preferred_element_type=jnp.float32
    )
    grad_probs = jnp.einsum(
        "psfhd,psehd->pshfe",
        grad_mixture,
        values.reshape(head_shape),
        preferred_element_type=jnp.float32,
    )
    grad_scores = to_low(
        softmaxed * (grad_probs - jnp.sum(softmaxed * grad_probs, axis=-1, keepdims=True))
    )
    grad_queries = to_low(
        (
            jnp.einsum(
                "pshfe,psehd->psfhd",
                grad_scores,
                key_vecs.reshape(head_shape),
                preferred_element_type=jnp.float32,
            )
            / math.sqrt(HEAD_DIM)
        ).reshape(queries.shape)
    )
    grad_keys = to_low(
        (
            jnp.einsum(
                "pshfe,psfhd->psehd",
                grad_scores,
                queries.reshape(head_shape),
                preferred_element_type=jnp.float32,
            )
            / math.sqrt(HEAD_DIM)
        ).reshape(queries.shape)
    )
    grad_values_low = to_low(grad_values.reshape(queries.shape))
    w_q_grad = contract(normal_a, grad_queries)
    w_k_grad = contract(normal_a, grad_keys)
    w_v_grad = contract(normal_a, grad_values_low)
    grad_normal_a = (
        product_back(grad_queries, squares[first])
        + product_back(grad_keys, squares[first + 1])
        + product_back(grad_values_low, squares[first + 2])
    )
    grad_ln, gain_grad, offset_grad = jax.vjp(layer_norm, stream, gain, offset)[1](grad_normal_a)
    return (
        grad_stream + grad_ln,
        (w_q_grad, w_k_grad, w_v_grad, w_o_grad),
        (gain_grad, offset_grad, b_o_grad),
    )


def motion_backward(grad_in, arrived, keep_video, low_weights, vectors, saved):
    squares, up_weight, down_weight = low_weights
    (
        inputs,
        motion_u,
        kept_first,
        middle,
        kept_second,
        upper,
        normal_c,
        gate_up,
        inner_act,
        final_low,
    ) = saved
    grad_branch = grad_in * to_low(keep_video)
    w_out_grad = contract(final_low, grad_branch)
    b_out_grad = column_sum(grad_branch)
    grad_last = product_back(grad_branch, squares[9])
    grad_ffn = to_low(grad_last)
    w_down_grad = contract(inner_act, grad_ffn)
    b_down_grad = column_sum(grad_ffn)
    grad_inner = product_back(grad_ffn, down_weight)
    grad_gate_up = to_low(jax.vjp(gated_gelu, gate_up)[1](grad_inner)[0])
    w_up_grad = contract(normal_c, grad_gate_up)
    grad_normal_c = product_back(grad_gate_up, up_weight)
    grad_upper_ln, g_ln3, b_ln3 = jax.vjp(layer_norm, upper, vectors[9], vectors[10])[1](
        grad_normal_c
    )
    grad_upper = grad_last + grad_upper_ln
    grad_middle, second_w, second_v = temporal_backward(
        grad_upper, middle, squares, 5, vectors[6], vectors[7], kept_second
    )
    grad_u_sum, first_w, first_v = temporal_backward(
        grad_middle, motion_u, squares, 1, vectors[3], vectors[4], kept_first
    )
    grad_motion_u = to_low(grad_u_sum)
    w_in_grad = contract(inputs, grad_motion_u)
    b_in_grad = column_sum(grad_motion_u)
    grad_inputs = product_back(grad_motion_u, squares[0])
    g_norm = jnp.sum(grad_inputs * arrived.astype(jnp.float32), axis=(0, 1, 2))
    b_norm = jnp.sum(grad_inputs, axis=(0, 1, 2))
    square_grads = jnp.stack(
        [
            w_in_grad,
            first_w[0],
            first_w[1],
            first_w[2],
            first_w[3],
            second_w[0],
            second_w[1],
            second_w[2],
            second_w[3],
            w_out_grad,
        ]
    )
    vector_grads = jnp.stack(
        [
            g_norm,
            b_norm,
            b_in_grad,
            first_v[0],
            first_v[1],
            first_v[2],
            second_v[0],
            second_v[1],
            second_v[2],
            g_ln3,
            b_ln3,
            b_down_grad,
            b_out_grad,
        ]
    )
    return (square_grads, w_up_grad, w_down_grad, vector_grads)


def orthogonalize(matrix):
    is_tall = matrix.shape[0] > matrix.shape[1]
    current = matrix.T if is_tall else matrix
    current = current / (jnp.sqrt(jnp.sum(current * current)) + 1e-07)
    for _ in range(5):
        gram_matrix = jnp.dot(current, current.T, precision=PRECISE)
        polynomial = -4.775 * gram_matrix + 2.0315 * jnp.dot(
            gram_matrix, gram_matrix, precision=PRECISE
        )
        current = 3.4445 * current + jnp.dot(polynomial, current, precision=PRECISE)
    return current.T if is_tall else current


def shards(
    latents,
    noise,
    timesteps,
    image_flags,
    frame_counts,
    text,
    conv_in,
    res_convs,
    conv_out,
    time_w1,
    time_w2,
    temb_w,
    spatial_squares,
    cross_kv,
    spatial_up,
    spatial_down,
    frozen_vectors,
    motion_squares,
    motion_up,
    motion_down,
    motion_vectors,
    square_moment,
    up_moment,
    down_moment,
    vector_moment1,
    vector_moment2,
    square_ema,
    up_ema,
    down_ema,
    vector_ema,
):
    frames_dev = latents.shape[1]
    samples_grp = timesteps.shape[1]
    frame_pos = lax.axis_index("frames") * frames_dev + jnp.arange(frames_dev)
    selector = (frame_pos[:, None] // CLIP == jnp.arange(samples_grp)[None, :]).astype(jnp.float32)
    step_values = jnp.sum(selector * timesteps[0].astype(jnp.float32)[None, :], axis=1)
    phases = (step_values / 1000.0 + 0.008) / 1.008 * (math.pi / 2)
    keep_rate = jnp.cos(phases)[:, None, None]
    noise_rate = jnp.sin(phases)[:, None, None]
    clean_latent = latents[0].astype(jnp.float32)
    drawn_noise = noise[0].astype(jnp.float32)
    noisy = keep_rate * clean_latent + noise_rate * drawn_noise
    target = keep_rate * drawn_noise - noise_rate * clean_latent
    temb_res = time_embed(step_values, time_w1, time_w2, temb_w, frozen_vectors[22])
    text_rows = jnp.einsum(
        "fs,sx->fx",
        to_low(selector),
        text[0].reshape(samples_grp, -1),
        preferred_element_type=jnp.float32,
    )
    text_rows = to_low(text_rows).reshape(frames_dev, TEXT_LEN, TEXT_DIM)
    frozen = (
        conv_in,
        res_convs,
        spatial_squares,
        cross_kv,
        spatial_up,
        spatial_down,
        frozen_vectors,
    )
    hidden = lax.map(
        lambda bundle: frame_forward(bundle[0], bundle[1], bundle[2], frozen),
        (noisy, temb_res, text_rows),
    )
    normed = to_low(group_norm(hidden, 1.0, 0.0))
    arrived = lax.all_to_all(
        jnp.swapaxes(normed, 0, 1), "frames", split_axis=0, concat_axis=1, tiled=True
    )
    pixels_dev = arrived.shape[0]
    arrived = arrived.reshape(pixels_dev, samples_grp, CLIP, WIDTH)
    group_counts = lax.dynamic_slice_in_dim(frame_counts, lax.axis_index("dp"), 1, 0)[0].astype(
        jnp.float32
    )
    valid_frames = (jnp.arange(CLIP, dtype=jnp.float32)[None, :] < group_counts[:, None]).astype(
        jnp.float32
    )
    masking = jnp.where(valid_frames > 0.5, 0.0, -1e30).astype(jnp.float32)
    keep_video = (1.0 - image_flags[0].astype(jnp.float32))[None, :, None, None]
    low_weights = (to_low(motion_squares), to_low(motion_up), to_low(motion_down))
    branch, saved = motion_forward(arrived, masking, keep_video, low_weights, motion_vectors)
    returned = lax.all_to_all(
        branch.reshape(pixels_dev, -1, WIDTH), "frames", split_axis=1, concat_axis=0, tiled=True
    )
    mixed_h = hidden + jnp.swapaxes(returned, 0, 1).astype(jnp.float32)

    def head_norm(values):
        return jax.nn.silu(group_norm(values, frozen_vectors[20], frozen_vectors[21]))

    activation, head_back = jax.vjp(head_norm, mixed_h)
    predicted = convolve(to_low(activation), conv_out)
    frame_limit = jnp.sum(selector * group_counts[None, :], axis=1)
    frame_valid = ((frame_pos % CLIP).astype(jnp.float32) < frame_limit).astype(jnp.float32)[
        :, None, None
    ]
    total_count = 4.0 * PIX * jnp.sum(frame_counts).astype(jnp.float32)
    residual = predicted - target
    loss_sum = lax.psum(jnp.sum(frame_valid * jnp.square(residual)), ("frames", "dp"))
    grad_pred = to_low(2.0 * (frame_valid * residual) / total_count)
    flipped = jnp.swapaxes(conv_out[::-1, ::-1], 2, 3)
    grad_mixed = head_back(convolve(grad_pred, flipped))[0]
    grad_in = lax.all_to_all(
        jnp.swapaxes(to_low(grad_mixed), 0, 1), "frames", split_axis=0, concat_axis=1, tiled=True
    )
    grad_in = grad_in.reshape(pixels_dev, samples_grp, CLIP, WIDTH)
    gradients = motion_backward(grad_in, arrived, keep_video, low_weights, motion_vectors, saved)
    gradients = lax.psum((gradients[0], gradients[1], gradients[2], gradients[3]), ("frames", "dp"))
    grad_sq, grad_up, grad_down, grad_vec = gradients
    dp_index = lax.axis_index("dp")
    half_sq = square_moment.shape[0]
    half_up = up_moment.shape[1]
    half_down = down_moment.shape[0]
    sq_moment_new = 0.95 * square_moment + lax.dynamic_slice_in_dim(
        grad_sq, dp_index * half_sq, half_sq, 0
    )
    up_moment_new = 0.95 * up_moment + lax.dynamic_slice_in_dim(
        grad_up, dp_index * half_up, half_up, 1
    )
    down_moment_new = 0.95 * down_moment + lax.dynamic_slice_in_dim(
        grad_down, dp_index * half_down, half_down, 0
    )
    nesterov = (
        lax.dynamic_slice_in_dim(grad_sq, dp_index * half_sq, half_sq, 0) + 0.95 * sq_moment_new,
        lax.dynamic_slice_in_dim(grad_up, dp_index * half_up, half_up, 1) + 0.95 * up_moment_new,
        lax.dynamic_slice_in_dim(grad_down, dp_index * half_down, half_down, 0)
        + 0.95 * down_moment_new,
    )
    full_sq, full_up, full_down = (
        lax.all_gather(nesterov[0], "dp", axis=0, tiled=True),
        lax.all_gather(nesterov[1], "dp", axis=1, tiled=True),
        lax.all_gather(nesterov[2], "dp", axis=0, tiled=True),
    )
    frame_index = lax.axis_index("frames")
    frame_count = lax.axis_size("frames")
    matrices = [full_sq[matrix_id] for matrix_id in range(10)] + [full_up, full_down]
    results = []
    for position, matrix in enumerate(matrices):
        owner_id = position * frame_count // len(matrices)
        results.append(lax.cond(frame_index == owner_id, orthogonalize, jnp.zeros_like, matrix))
    directions = lax.psum((jnp.stack(results[:10]), results[10], results[11]), "frames")
    shrink = 1.0 - MUON_RATE * DECAY
    square_new = motion_squares * shrink - MUON_RATE * 0.2 * math.sqrt(WIDTH) * directions[0]
    up_new = (
        motion_up * shrink - MUON_RATE * 0.2 * math.sqrt(max(WIDTH, 2 * FF_INNER)) * directions[1]
    )
    down_new = (
        motion_down * shrink - MUON_RATE * 0.2 * math.sqrt(max(FF_INNER, WIDTH)) * directions[2]
    )
    square_ema_new = AVERAGE * square_ema + (1.0 - AVERAGE) * lax.dynamic_slice_in_dim(
        square_new, dp_index * half_sq, half_sq, 0
    )
    up_ema_new = AVERAGE * up_ema + (1.0 - AVERAGE) * lax.dynamic_slice_in_dim(
        up_new, dp_index * half_up, half_up, 1
    )
    down_ema_new = AVERAGE * down_ema + (1.0 - AVERAGE) * lax.dynamic_slice_in_dim(
        down_new, dp_index * half_down, half_down, 0
    )
    moment_first = 0.9 * vector_moment1 + 0.1 * grad_vec
    moment_second = 0.999 * vector_moment2 + 0.001 * jnp.square(grad_vec)
    adjusted = (
        moment_first / (1.0 - 0.9**STEP) / (jnp.sqrt(moment_second / (1.0 - 0.999**STEP)) + 1e-08)
    )
    vector_new = motion_vectors - ADAM_RATE * (adjusted + DECAY * motion_vectors)
    return (
        loss_sum,
        total_count,
        square_new,
        sq_moment_new,
        square_ema_new,
        up_new,
        up_moment_new,
        up_ema_new,
        down_new,
        down_moment_new,
        down_ema_new,
        moment_first,
        moment_second,
        vector_new,
        AVERAGE * vector_ema + (1.0 - AVERAGE) * vector_new,
    )


def solution(mesh):
    return jax.shard_map(
        shards,
        mesh=mesh,
        in_specs=(
            P("dp", "frames", None, None),
            P("dp", "frames", None, None),
            P("dp", None),
            P("dp", None),
            P(),
            P("dp", None, None, None),
            P(),
            P(),
            P(),
            P(),
            P(),
            P(),
            P(),
            P(),
            P(),
            P(),
            P(),
            P(),
            P(),
            P(),
            P(),
            P("dp", None, None),
            P(None, "dp"),
            P("dp", None),
            P(),
            P(),
            P("dp", None, None),
            P(None, "dp"),
            P("dp", None),
            P(),
        ),
        out_specs=(
            P(),
            P(),
            P(),
            P("dp", None, None),
            P("dp", None, None),
            P(),
            P(None, "dp"),
            P(None, "dp"),
            P(),
            P("dp", None),
            P("dp", None),
            P(),
            P(),
            P(),
            P(),
        ),
        check_vma=False,
    )
```

profile of v0, /device:TPU:0, one launch (start us, length us, event | category | flops | bytes accessed | tf_op | source)
XLA Modules:
  0.0 1251.9 jit_solution(6868908222452782654)
XLA Ops:
  33.0 8.0 select_reduce_fusion.1
  53.9 17.6 %fusion.437 = (f32[8,1024]{1,0:T(8,128)S(1)}, f32[8,1024,1024]{1,2,0:T(8,128)}) fusion(bf16[1024,8,40]{0,2,1:T(8,128)(2,1)} %bitcast.925, bf16[1024,8,40]{0,2,1:T(8,128)(2,1)} %bitcast.926), kind=kOutput, calls=%fused_computation.815 | convolution fusion | flops 696255488 | bytes 34897920 | tf_op jit(solution)/shard_map/while/body/eval_jaxpr/sub | solution.py:87
  71.6 12.4 fusion.215
  115.3 16.8 %fusion.441 = (f32[320]{0:T(512)S(1)}, f32[1024,320]{0,1:T(8,128)S(1)}) fusion(f32[320]{0:T(512)S(1)} %get-tuple-element.146, bf16[8,320,320]{2,1,0:T(8,128)(2,1)} %param.66, f32[1024,320]{0,1:T(8,128)S(1)} %get-tuple-element.245, bf16[1280,320]{0,1:T(8,128)(2,1)} %param.69, f32[1024,2560]{1,0:T(8,128)} %fusion.261, f32[320]{0:T(512)S(1)} %get-tuple-element.145, ...), kind=kOutput, calls=%fused_computation.819 | convolution fusion | flops 1138032384 | bytes 16800000 | tf_op jit(solution)/shard_map/while/body/eval_jaxpr/...i,ij->...j/dot_general | solution.py:33
  137.1 8.5 all-to-all-start
  151.9 11.0 all-to-all-done
  255.8 12.7 %fusion.151 = (bf16[64,16,1280]{2,1,0:T(8,128)(2,1)S(1)}, f32[64,1,16,1280]{3,2,0,1:T(8,128)}) fusion(f32[64,1,16,2560]{3,2,0,1:T(8,128)S(1)} %convolution_bitcast_fusion), kind=kLoop, calls=%fused_computation.354 | loop fusion | flops 86507520 | bytes 18350080 | tf_op jit(solution)/shard_map/reshape.189
  279.8 16.6 %all-to-all-done.1 = bf16[64,16,320]{2,0,1:T(8,128)(2,1)} async-done(((bf16[64,16,320]{2,0,1:T(8,128)(2,1)}), bf16[64,16,320]{2,0,1:T(8,128)(2,1)}, u32[]{:S(2)}, u32[]{:S(2)}) %all-to-all-start.1) | async-done | bytes 655392 | tf_op jit(solution)/shard_map/all_to_all | solution.py:429
  306.9 20.8 %fusion.230 = f32[32,8,5,4]{1,3,2,0:T(4,128)} fusion(bf16[3,3,320,4]{2,3,1,0:T(4,128)(2,1)S(1)} %copy-done.117, bf16[32,1,7,2,320]{4,2,3,0,1:T(8,128)(2,1)S(1)} %slice.379, bf16[32,1,8,5,320]{4,2,3,0,1:T(8,128)(2,1)S(1)} %copy.438, pred[8,5]{0,1:T(8,128)(4,1)S(1)} %copy-done.91), kind=kOutput, calls=%fused_computation.526 | convolution fusion | flops 32322560 | bytes 1149480 | tf_op jit(solution)/shard_map/conv_general_dilated | solution.py:43
  358.0 15.2 %all-to-all-done.2 = bf16[16,2,10240]{2,1,0:T(2,128)(2,1)} async-done(((bf16[16,2,10240]{2,1,0:T(2,128)(2,1)}), bf16[16,2,10240]{2,1,0:T(2,128)(2,1)}, u32[]{:S(2)}, u32[]{:S(2)}) %all-to-all-start.2) | async-done | bytes 655392 | tf_op jit(solution)/shard_map/all_to_all | solution.py:449
  522.7 194.9 %all-reduce.8.cloned.1.call-done = (f32[10,320,320]{2,1,0:T(8,128)}, f32[320,2560]{1,0:T(8,128)}, f32[1280,320]{0,1:T(8,128)}) async-done(((f32[10,320,320]{2,1,0:T(8,128)}, f32[320,2560]{1,0:T(8,128)}, f32[1280,320]{0,1:T(8,128)}), (f32[10,320,320]{2,1,0:T(8,128)}, f32[320,2560]{1,0:T(8,128)}, f32[1280,320]{0,1:T(8,128)})) %all-reduce.8.cloned.1.call-update) | async-done | bytes 9011216 | tf_op jit(solution)/shard_map/psum | solution.py:454
  730.1 10.2 conditional.23
  745.9 11.4 conditional.22
  763.8 25.5 %conditional.12 = (f32[1,320,320]{2,1,0:T(8,128)S(1)}) conditional(s32[]{:T(128)} %convert_element_type.667, () %tuple.104, f32[10,320,320]{2,1,0:T(8,128)} %all-gather.4.cloned.1.call-done), branch_computations={%region_61.62_spmd, %region_62.64_spmd} | conditional | flops 5901312000 | bytes 15402020 | solution.py:486
  790.1 11.6 conditional.13
  802.6 11.8 conditional.14
  815.3 11.6 conditional.15
  827.7 11.8 conditional.16
  840.4 11.6 conditional.17
  852.8 11.8 conditional.18
  865.5 11.6 conditional.19
  878.0 11.8 conditional.20
  898.9 80.1 %all-reduce.2 = (f32[]{:T(128)}, f32[13,320]{1,0:T(8,128)S(1)}) all-reduce(f32[]{:T(128)} %get-tuple-element.226, f32[13,320]{1,0:T(8,128)S(1)} %stack.173), channel_id=1, replica_groups=mesh['frames'=16,'dp'=2] {'frames','dp'}, use_global_device_ids=true, to_apply=%region_41.42 | all-reduce | flops 4161 | bytes 33288 | tf_op jit(solution)/shard_map/psum | solution.py:445
  979.6 247.4 %all-reduce.10.cloned.1.call-done = (f32[10,320,320]{2,1,0:T(8,128)}, f32[320,2560]{1,0:T(8,128)}, f32[1280,320]{0,1:T(8,128)}) async-done(((f32[10,320,320]{2,1,0:T(8,128)}, f32[320,2560]{1,0:T(8,128)}, f32[1280,320]{0,1:T(8,128)}), (f32[10,320,320]{2,1,0:T(8,128)}, f32[320,2560]{1,0:T(8,128)}, f32[1280,320]{0,1:T(8,128)})) %all-reduce.10.cloned.1.call-update) | async-done | bytes 9011216 | tf_op jit(solution)/shard_map/psum | solution.py:487
  (598 shorter events, 453.0 us)
Async XLA Ops:
  7.2 14.9 %copy-start = (bf16[1280,1280]{1,0:T(8,128)(2,1)S(1)}, bf16[1280,1280]{1,0:T(8,128)(2,1)}, u32[]{:S(2)}) copy-start(bf16[1280,1280]{1,0:T(8,128)(2,1)} %param.64) | copy-start | bytes 9830404
  53.9 17.6 %copy-start.75 = (bf16[1024,320]{0,1:T(8,128)(2,1)S(1)}, bf16[1024,320]{0,1:T(8,128)(2,1)}, u32[]{:S(2)}) copy-start(bf16[1024,320]{0,1:T(8,128)(2,1)} %convolution_convert_fusion.12) | copy-start | bytes 1966084
  137.1 25.9 %all-to-all-start = ((bf16[16,2,10240]{2,1,0:T(2,128)(2,1)}), bf16[16,2,10240]{2,1,0:T(2,128)(2,1)S(1)}, u32[]{:S(2)}, u32[]{:S(2)}) async-start(bf16[16,2,10240]{2,1,0:T(2,128)(2,1)} %reshape.1919), calls=%async_computation | async-start | bytes 1310720 | tf_op jit(solution)/shard_map/all_to_all | solution.py:414
  151.8 12.8 %copy-start.97 = (f32[320]{0:T(512)}, f32[320]{0:T(512)S(1)}, u32[]{:S(2)}) copy-start(f32[320]{0:T(512)S(1)} %get-tuple-element.178) | copy-start | bytes 3844
  151.8 12.8 %copy-start.99 = (f32[320]{0:T(512)}, f32[320]{0:T(512)S(1)}, u32[]{:S(2)}) copy-start(f32[320]{0:T(512)S(1)} %get-tuple-element.179) | copy-start | bytes 3844
  151.8 15.4 %copy-start.88 = (f32[320]{0:T(512)}, f32[320]{0:T(512)S(1)}, u32[]{:S(2)}) copy-start(f32[320]{0:T(512)S(1)} %get-tuple-element.176) | copy-start | bytes 3844
  166.7 40.7 %copy-start.2 = (f32[64,16,320]{2,1,0:T(8,128)}, f32[64,16,320]{2,1,0:T(8,128)S(1)}, u32[]{:S(2)}) copy-start(f32[64,16,320]{2,1,0:T(8,128)S(1)} %get-tuple-element.249) | copy-start | bytes 3932164
  252.4 16.1 %copy-start.5 = (f32[64,16,320]{2,1,0:T(8,128)}, f32[64,16,320]{2,1,0:T(8,128)S(1)}, u32[]{:S(2)}) copy-start(f32[64,16,320]{2,1,0:T(8,128)S(1)} %get-tuple-element.257) | copy-start | bytes 3932164
  255.7 12.7 %copy-start.4 = (f32[64,1,16,2560]{3,2,0,1:T(8,128)}, f32[64,1,16,2560]{3,2,0,1:T(8,128)S(1)}, u32[]{:S(2)}) copy-start(f32[64,1,16,2560]{3,2,0,1:T(8,128)S(1)} %convolution_bitcast_fusion) | copy-start | bytes 31457284
  255.7 12.7 %copy-start.62 = (f32[1280,320]{0,1:T(8,128)S(1)}, f32[1280,320]{0,1:T(8,128)}, u32[]{:S(2)}) copy-start(f32[1280,320]{0,1:T(8,128)} %param.73) | copy-start | bytes 4915204
  273.0 23.4 %all-to-all-start.1 = ((bf16[64,16,320]{2,0,1:T(8,128)(2,1)}), bf16[64,16,320]{2,0,1:T(8,128)(2,1)}, u32[]{:S(2)}, u32[]{:S(2)}) async-start(bf16[64,16,320]{2,0,1:T(8,128)(2,1)} %copy.433), calls=%async_computation.1 | async-start | bytes 1572864 | tf_op jit(solution)/shard_map/all_to_all | solution.py:429
  346.2 10.5 copy-start.9
  351.7 21.5 %all-to-all-start.2 = ((bf16[16,2,10240]{2,1,0:T(2,128)(2,1)}), bf16[16,2,10240]{2,1,0:T(2,128)(2,1)}, u32[]{:S(2)}, u32[]{:S(2)}) async-start(bf16[16,2,10240]{2,1,0:T(2,128)(2,1)} %reshape.1921), calls=%async_computation.2 | async-start | bytes 1310720 | tf_op jit(solution)/shard_map/all_to_all | solution.py:449
  356.7 360.9 %all-reduce.8.cloned.1.call-start = ((), (), s32[]{:S(2)}) async-start(), calls=%async_computation.6 | async-start | bytes 19660800 | tf_op jit(solution)/shard_map/psum | solution.py:454
  489.5 7.1 copy-start.89
  522.6 195.0 %copy-start.72 = (f32[640,320]{0,1:T(8,128)S(1)}, f32[640,320]{0,1:T(8,128)}, u32[]{:S(2)}) copy-start(f32[640,320]{0,1:T(8,128)} %param.77) | copy-start | bytes 2457604
  522.6 207.5 %all-gather.8.cloned.1.call-start = ((), (), s32[]{:S(2)}) async-start(), calls=%async_computation.5 | async-start | bytes 2457600 | tf_op jit(solution)/shard_map/all_gather | solution.py:478
  720.0 25.8 %all-gather.6.cloned.1.call-start = ((), (), s32[]{:S(2)}) async-start(), calls=%async_computation.4 | async-start | bytes 4915200 | tf_op jit(solution)/shard_map/all_gather | solution.py:477
  724.2 39.6 %all-gather.4.cloned.1.call-start = ((), (), s32[]{:S(2)}) async-start(), calls=%async_computation.3 | async-start | bytes 7372800 | tf_op jit(solution)/shard_map/all_gather | solution.py:476
  728.7 498.4 %all-reduce.10.cloned.1.call-start = ((), (), s32[]{:S(2)}) async-start(), calls=%async_computation.7 | async-start | bytes 19660800 | tf_op jit(solution)/shard_map/psum | solution.py:487
  898.0 81.0 %copy-start.86 = (f32[13,320]{1,0:T(8,128)S(1)}, f32[13,320]{1,0:T(8,128)}, u32[]{:S(2)}) copy-start(f32[13,320]{1,0:T(8,128)} %param.74) | copy-start | bytes 49924
  898.0 81.0 %copy-start.92 = (f32[13,320]{1,0:T(8,128)S(1)}, f32[13,320]{1,0:T(8,128)}, u32[]{:S(2)}) copy-start(f32[13,320]{1,0:T(8,128)} %param.83) | copy-start | bytes 49924
  898.0 81.0 %copy-start.93 = (f32[13,320]{1,0:T(8,128)S(1)}, f32[13,320]{1,0:T(8,128)}, u32[]{:S(2)}) copy-start(f32[13,320]{1,0:T(8,128)} %param.79) | copy-start | bytes 49924
  898.0 80.9 %copy-start.94 = (f32[13,320]{1,0:T(8,128)S(1)}, f32[13,320]{1,0:T(8,128)}, u32[]{:S(2)}) copy-start(f32[13,320]{1,0:T(8,128)} %param.78) | copy-start | bytes 49924
  (105 other events, 272.0 us)
Sparse Core Ops, SparseCore 0:
  522.7 194.7 all-reduce.7
  720.2 9.9 all-gather.7
  732.3 13.4 all-gather.5
  747.9 15.8 all-gather.3
  898.2 328.8 all-reduce.9
where the time goes:
time: 1260 us; the launch traced here: 1250 us
  waiting for transfers between devices  499 us (40%)
  matrix products  257 us (20%)
  local copies, waits for them, and re-layouts  167 us (13%)
  loops' own time  123 us (10%)
  other arithmetic  87.7 us (7%)
  blocking collectives  80.1 us (6%)
  between operations  20.4 us (2%)
  starting transfers between devices  18.3 us (1%)
    psum x1, waiting for transfers between devices, shards(): lax.psum((jnp.stack(results[:10]), results[10], results[11]), 'frames')  247 us
    psum x1, waiting for transfers between devices, shards(): lax.psum((gradients[0], gradients[1], gradients[2], gradients[3]), ('fram...  195 us
    another operation x12, loops' own time, shards(): lax.cond(frame_index == owner_id, orthogonalize, jnp.zeros_like, matrix)  123 us
    psum x1, blocking collectives, shards(): lax.psum(jnp.sum(frame_valid * jnp.square(residual)), ('frames', 'dp'))  80.1 us
    dot_general x25, matrix products, product(): jnp.einsum('...i,ij->...j', left, right, preferred_element_type=jnp.float32)  62.9 us
    convert_element_type x37, local copies, waits for them, and re-layouts, to_low(): return values.astype(jnp.bfloat16)  62.5 us
    unnamed x258, local copies, waits for them, and re-layouts  39.8 us
    conv_general_dilated x5, matrix products, convolve(): lax.conv_general_dilated(images, kernel, (1, 1), 'SAME', dimension_number...  37.4 us
  transfers between devices with their start and end apart: 8, of which 8 were waited for; matrix products, arithmetic and copies ran while one was open for 2% of the time, Pallas kernels for 0%

commit v1 on v0

--- a/solution.py
+++ b/solution.py
@@ -3,6 +3,8 @@
 import jax
 import jax.numpy as jnp
 from jax import lax
+from jax.experimental import pallas as pl
+from jax.experimental.pallas import tpu as pltpu
 from jax.sharding import PartitionSpec as P
 
 WIDTH = 320
@@ -332,17 +334,165 @@
     return (square_grads, w_up_grad, w_down_grad, vector_grads)
 
 
-def orthogonalize(matrix):
-    is_tall = matrix.shape[0] > matrix.shape[1]
-    current = matrix.T if is_tall else matrix
-    current = current / (jnp.sqrt(jnp.sum(current * current)) + 1e-07)
-    for _ in range(5):
-        gram_matrix = jnp.dot(current, current.T, precision=PRECISE)
-        polynomial = -4.775 * gram_matrix + 2.0315 * jnp.dot(
-            gram_matrix, gram_matrix, precision=PRECISE
+F32 = jnp.float32
+BF16 = jnp.bfloat16
+VMEM_LIMIT = 56 * 2**20
+HALF = CLIP // 2
+
+
+def in_vmem():
+    return pl.BlockSpec(memory_space=pltpu.VMEM)
+
+
+def halves(values):
+    high = values.astype(BF16)
+    return (high, (values - high.astype(F32)).astype(BF16))
+
+
+def triple(left, right, transposed=False):
+    stacked = jnp.concatenate([left[0], left[0], left[1]], axis=1)
+    if transposed:
+        other = jnp.concatenate([right[0], right[1], right[0]], axis=1)
+        dims = (((1,), (1,)), ((), ()))
+    else:
+        other = jnp.concatenate([right[0], right[1], right[0]], axis=0)
+        dims = (((1,), (0,)), ((), ()))
+    return lax.dot_general(stacked, other, dims, preferred_element_type=F32)
+
+
+def scaled_to_unit(matrix):
+    return matrix * (1.0 / (jnp.sqrt(jnp.sum(matrix * matrix, keepdims=True)) + 1e-07))
+
+
+def square_directions_kernel(x_ref, o_ref):
+    count = x_ref.shape[0]
+    for index in range(count):
+        o_ref[index] = scaled_to_unit(x_ref[index])
+
+    def step(_, carry):
+        for index in range(count):
+            current = o_ref[index]
+            parts = halves(current)
+            gram = triple(parts, parts, True)
+            gram_parts = halves(gram)
+            polynomial = -4.775 * gram + 2.0315 * triple(gram_parts, gram_parts)
+            o_ref[index] = 3.4445 * current + triple(halves(polynomial), parts)
+        return carry
+
+    lax.fori_loop(0, 5, step, 0)
+
+
+def square_directions(matrices):
+    return pl.pallas_call(
+        square_directions_kernel,
+        out_shape=jax.ShapeDtypeStruct(matrices.shape, F32),
+        in_specs=[in_vmem()],
+        out_specs=in_vmem(),
+        compiler_params=pltpu.CompilerParams(vmem_limit_bytes=VMEM_LIMIT),
+        name="square_directions",
+    )(matrices)
+
+
+def wide_direction_kernel(x_ref, o_ref):
+    parts = halves(scaled_to_unit(x_ref[...]))
+    gram = triple(parts, parts, True)
+    size = gram.shape[0]
+    total = None
+    for step in range(5):
+        gram_parts = halves(gram)
+        polynomial = -4.775 * gram + 2.0315 * triple(gram_parts, gram_parts)
+        poly_parts = halves(polynomial)
+        if total is None:
+            row = lax.broadcasted_iota(jnp.int32, (size, size), 0)
+            column = lax.broadcasted_iota(jnp.int32, (size, size), 1)
+            total = polynomial + jnp.where(row == column, 3.4445, 0.0)
+        else:
+            total = 3.4445 * total + triple(poly_parts, halves(total))
+        if step < 4:
+            once = 3.4445 * gram + triple(poly_parts, gram_parts)
+            gram = 3.4445 * once + triple(halves(once), poly_parts)
+    o_ref[...] = triple(halves(total), parts)
+
+
+def wide_direction(matrix):
+    return pl.pallas_call(
+        wide_direction_kernel,
+        out_shape=jax.ShapeDtypeStruct(matrix.shape, F32),
+        in_specs=[in_vmem()],
+        out_specs=in_vmem(),
+        compiler_params=pltpu.CompilerParams(vmem_limit_bytes=VMEM_LIMIT),
+        name="wide_direction",
+    )(matrix)
+
+
+def swap_cores(values):
+    return lax.ppermute(values, "dp", [(0, 1), (1, 0)])
+
+
+def frames_bit(bit):
+    return (lax.axis_index("frames") // bit) % 2
+
+
+def swap_frames(values, bit):
+    size = lax.axis_size("frames")
+    return lax.ppermute(values, "frames", [(i, i ^ bit) for i in range(size)])
+
+
+def sum_over_frames(values, order):
+    for bit in order:
+        rows = values.shape[0] // 2
+        mine = frames_bit(bit)
+        own = lax.dynamic_slice_in_dim(values, mine * rows, rows, 0)
+        other = lax.dynamic_slice_in_dim(values, (1 - mine) * rows, rows, 0)
+        values = own + swap_frames(other, bit)
+    for bit in reversed(order):
+        got = swap_frames(values, bit)
+        values = jnp.where(
+            frames_bit(bit) == 0,
+            jnp.concatenate([values, got], 0),
+            jnp.concatenate([got, values], 0),
         )
-        current = 3.4445 * current + jnp.dot(polynomial, current, precision=PRECISE)
-    return current.T if is_tall else current
+    return values
+
+
+def sum_rows(values):
+    size = lax.axis_size("frames")
+    bits = []
+    bit = 1
+    while bit < size:
+        bits.append(bit)
+        bit *= 2
+    unit = 8 * size
+    rows = values.shape[0]
+    padded = -(-rows // unit) * unit
+    values = jnp.pad(values, ((0, padded - rows), (0, 0)))
+    cut = (padded // unit + 1) // 2 * unit
+    first = sum_over_frames(values[:cut], bits)
+    second = sum_over_frames(values[cut:], [bits[1], bits[0]] + bits[2:])
+    return jnp.concatenate([first, second], 0)[:rows]
+
+
+def sample_groups():
+    groups = []
+    for block in range(lax.axis_size("frames") // CLIP):
+        for half in range(2):
+            groups.append(
+                [
+                    2 * (block * CLIP + half * HALF + place) + core
+                    for core in range(2)
+                    for place in range(HALF)
+                ]
+            )
+    return groups
+
+
+def swap_samples(values):
+    size = lax.axis_size("frames")
+    pairs = []
+    for frame in range(size):
+        half = (frame % CLIP) // HALF
+        pairs.append((2 * frame + 1 - half, 2 * (frame ^ HALF) + half))
+    return lax.ppermute(values, ("frames", "dp"), pairs)
 
 
 def shards(
@@ -377,26 +527,36 @@
     down_ema,
     vector_ema,
 ):
-    frames_dev = latents.shape[1]
-    samples_grp = timesteps.shape[1]
-    frame_pos = lax.axis_index("frames") * frames_dev + jnp.arange(frames_dev)
-    selector = (frame_pos[:, None] // CLIP == jnp.arange(samples_grp)[None, :]).astype(jnp.float32)
-    step_values = jnp.sum(selector * timesteps[0].astype(jnp.float32)[None, :], axis=1)
+    dp_index = lax.axis_index("dp")
+    place = lax.axis_index("frames")
+    block = place // CLIP
+    place = place % CLIP
+    half = place // HALF
+    stays = half == dp_index
+    frame = jnp.where(stays, place, (place + HALF) % CLIP)
+    pair = jnp.concatenate([latents.reshape(64, 64), noise.reshape(64, 64)], axis=1)
+    pair = jnp.where(stays, pair, swap_samples(pair))
+    clean_latent = pair[:, :64].reshape(1, PIX, 4).astype(jnp.float32)
+    drawn_noise = pair[:, 64:].reshape(1, PIX, 4).astype(jnp.float32)
+
+    def of_block(values):
+        return lax.dynamic_index_in_dim(values[0], block, 0, keepdims=False)
+
+    step_count = of_block(timesteps)
+    facts = jnp.stack([step_count // 32, step_count % 32, of_block(image_flags)])
+    facts = jnp.pad(facts.astype(jnp.bfloat16)[None, :], ((0, 0), (0, TEXT_DIM - 3)))
+    text_facts = jnp.concatenate([of_block(text), facts], axis=0)
+    text_facts = jnp.where(stays, text_facts, swap_cores(text_facts))
+    text_rows = text_facts[None, :TEXT_LEN]
+    facts = text_facts[TEXT_LEN].astype(jnp.float32)
+    step_values = (facts[0] * 32.0 + facts[1])[None]
+    flag = facts[2]
     phases = (step_values / 1000.0 + 0.008) / 1.008 * (math.pi / 2)
     keep_rate = jnp.cos(phases)[:, None, None]
     noise_rate = jnp.sin(phases)[:, None, None]
-    clean_latent = latents[0].astype(jnp.float32)
-    drawn_noise = noise[0].astype(jnp.float32)
     noisy = keep_rate * clean_latent + noise_rate * drawn_noise
     target = keep_rate * drawn_noise - noise_rate * clean_latent
     temb_res = time_embed(step_values, time_w1, time_w2, temb_w, frozen_vectors[22])
-    text_rows = jnp.einsum(
-        "fs,sx->fx",
-        to_low(selector),
-        text[0].reshape(samples_grp, -1),
-        preferred_element_type=jnp.float32,
-    )
-    text_rows = to_low(text_rows).reshape(frames_dev, TEXT_LEN, TEXT_DIM)
     frozen = (
         conv_in,
         res_convs,
@@ -406,28 +566,36 @@
         spatial_down,
         frozen_vectors,
     )
-    hidden = lax.map(
-        lambda bundle: frame_forward(bundle[0], bundle[1], bundle[2], frozen),
-        (noisy, temb_res, text_rows),
-    )
+    hidden = frame_forward(noisy[0], temb_res, text_rows[0], frozen)[None]
     normed = to_low(group_norm(hidden, 1.0, 0.0))
-    arrived = lax.all_to_all(
-        jnp.swapaxes(normed, 0, 1), "frames", split_axis=0, concat_axis=1, tiled=True
-    )
+    groups = sample_groups()
+
+    def to_positions(values):
+        return lax.all_to_all(
+            jnp.swapaxes(values, 0, 1),
+            ("frames", "dp"),
+            split_axis=0,
+            concat_axis=1,
+            tiled=True,
+            axis_index_groups=groups,
+        )
+
+    arrived = to_positions(normed)
     pixels_dev = arrived.shape[0]
-    arrived = arrived.reshape(pixels_dev, samples_grp, CLIP, WIDTH)
-    group_counts = lax.dynamic_slice_in_dim(frame_counts, lax.axis_index("dp"), 1, 0)[0].astype(
-        jnp.float32
-    )
-    valid_frames = (jnp.arange(CLIP, dtype=jnp.float32)[None, :] < group_counts[:, None]).astype(
-        jnp.float32
-    )
+    arrived = arrived.reshape(pixels_dev, 1, CLIP, WIDTH)
+    count = lax.dynamic_slice(frame_counts, (half, block), (1, 1))[0, 0].astype(jnp.float32)
+    valid_frames = (jnp.arange(CLIP, dtype=jnp.float32)[None, :] < count).astype(jnp.float32)
     masking = jnp.where(valid_frames > 0.5, 0.0, -1e30).astype(jnp.float32)
-    keep_video = (1.0 - image_flags[0].astype(jnp.float32))[None, :, None, None]
+    keep_video = jnp.full((1, 1, 1, 1), 1.0 - flag)
     low_weights = (to_low(motion_squares), to_low(motion_up), to_low(motion_down))
     branch, saved = motion_forward(arrived, masking, keep_video, low_weights, motion_vectors)
     returned = lax.all_to_all(
-        branch.reshape(pixels_dev, -1, WIDTH), "frames", split_axis=1, concat_axis=0, tiled=True
+        branch.reshape(pixels_dev, CLIP, WIDTH),
+        ("frames", "dp"),
+        split_axis=1,
+        concat_axis=0,
+        tiled=True,
+        axis_index_groups=groups,
     )
     mixed_h = hidden + jnp.swapaxes(returned, 0, 1).astype(jnp.float32)
 
@@ -436,55 +604,76 @@
 
     activation, head_back = jax.vjp(head_norm, mixed_h)
     predicted = convolve(to_low(activation), conv_out)
-    frame_limit = jnp.sum(selector * group_counts[None, :], axis=1)
-    frame_valid = ((frame_pos % CLIP).astype(jnp.float32) < frame_limit).astype(jnp.float32)[
-        :, None, None
-    ]
+    frame_valid = (frame.astype(jnp.float32) < count).astype(jnp.float32)
     total_count = 4.0 * PIX * jnp.sum(frame_counts).astype(jnp.float32)
     residual = predicted - target
-    loss_sum = lax.psum(jnp.sum(frame_valid * jnp.square(residual)), ("frames", "dp"))
+    loss_part = jnp.sum(frame_valid * jnp.square(residual))
     grad_pred = to_low(2.0 * (frame_valid * residual) / total_count)
     flipped = jnp.swapaxes(conv_out[::-1, ::-1], 2, 3)
     grad_mixed = head_back(convolve(grad_pred, flipped))[0]
-    grad_in = lax.all_to_all(
-        jnp.swapaxes(to_low(grad_mixed), 0, 1), "frames", split_axis=0, concat_axis=1, tiled=True
-    )
-    grad_in = grad_in.reshape(pixels_dev, samples_grp, CLIP, WIDTH)
-    gradients = motion_backward(grad_in, arrived, keep_video, low_weights, motion_vectors, saved)
-    gradients = lax.psum((gradients[0], gradients[1], gradients[2], gradients[3]), ("frames", "dp"))
-    grad_sq, grad_up, grad_down, grad_vec = gradients
-    dp_index = lax.axis_index("dp")
+    grad_in = to_positions(to_low(grad_mixed))
+    grad_in = grad_in.reshape(pixels_dev, 1, CLIP, WIDTH)
+    grad_sq, grad_up, grad_down, grad_vec = motion_backward(
+        grad_in, arrived, keep_video, low_weights, motion_vectors, saved
+    )
     half_sq = square_moment.shape[0]
     half_up = up_moment.shape[1]
     half_down = down_moment.shape[0]
-    sq_moment_new = 0.95 * square_moment + lax.dynamic_slice_in_dim(
-        grad_sq, dp_index * half_sq, half_sq, 0
-    )
-    up_moment_new = 0.95 * up_moment + lax.dynamic_slice_in_dim(
-        grad_up, dp_index * half_up, half_up, 1
-    )
-    down_moment_new = 0.95 * down_moment + lax.dynamic_slice_in_dim(
-        grad_down, dp_index * half_down, half_down, 0
-    )
-    nesterov = (
-        lax.dynamic_slice_in_dim(grad_sq, dp_index * half_sq, half_sq, 0) + 0.95 * sq_moment_new,
-        lax.dynamic_slice_in_dim(grad_up, dp_index * half_up, half_up, 1) + 0.95 * up_moment_new,
-        lax.dynamic_slice_in_dim(grad_down, dp_index * half_down, half_down, 0)
-        + 0.95 * down_moment_new,
-    )
-    full_sq, full_up, full_down = (
-        lax.all_gather(nesterov[0], "dp", axis=0, tiled=True),
-        lax.all_gather(nesterov[1], "dp", axis=1, tiled=True),
-        lax.all_gather(nesterov[2], "dp", axis=0, tiled=True),
-    )
-    frame_index = lax.axis_index("frames")
-    frame_count = lax.axis_size("frames")
-    matrices = [full_sq[matrix_id] for matrix_id in range(10)] + [full_up, full_down]
-    results = []
-    for position, matrix in enumerate(matrices):
-        owner_id = position * frame_count // len(matrices)
-        results.append(lax.cond(frame_index == owner_id, orthogonalize, jnp.zeros_like, matrix))
-    directions = lax.psum((jnp.stack(results[:10]), results[10], results[11]), "frames")
+    vector_part = jnp.concatenate([grad_vec.reshape(-1), loss_part[None]])
+    vector_part = jnp.pad(vector_part, (0, 64 * 128 - vector_part.shape[0])).reshape(64, 128)
+
+    def half_of(core):
+        return jnp.concatenate(
+            [
+                lax.dynamic_slice_in_dim(grad_sq, core * half_sq, half_sq, 0).reshape(-1, 128),
+                lax.dynamic_slice_in_dim(grad_up, core * half_up, half_up, 1).reshape(-1, 128),
+                lax.dynamic_slice_in_dim(grad_down, core * half_down, half_down, 0).reshape(-1, 128),
+                vector_part,
+            ],
+            axis=0,
+        )
+
+    summed = sum_rows(half_of(dp_index) + swap_cores(half_of(1 - dp_index)))
+    rows_sq = half_sq * WIDTH * WIDTH // 128
+    rows_up = WIDTH * half_up // 128
+    rows_down = WIDTH * half_down // 128
+    sum_sq = summed[:rows_sq].reshape(square_moment.shape)
+    sum_up = summed[rows_sq : rows_sq + rows_up].reshape(up_moment.shape)
+    sum_down = summed[rows_sq + rows_up : rows_sq + rows_up + rows_down].reshape(down_moment.shape)
+    vector_part = summed[rows_sq + rows_up + rows_down :].reshape(-1)
+    grad_vec = vector_part[: grad_vec.size].reshape(grad_vec.shape)
+    loss_sum = vector_part[grad_vec.size]
+    sq_moment_new = 0.95 * square_moment + sum_sq
+    up_moment_new = 0.95 * up_moment + sum_up
+    down_moment_new = 0.95 * down_moment + sum_down
+    own_up = sum_up + 0.95 * up_moment_new
+    own_down = jnp.pad((sum_down + 0.95 * down_moment_new).T, ((0, 0), (0, half_up - half_down)))
+    first_core = dp_index == 0
+    kept = jnp.where(first_core, own_up, own_down)
+    got = swap_cores(jnp.where(first_core, own_down, own_up))
+    wide = jnp.where(
+        first_core, jnp.concatenate([kept, got], 1), jnp.concatenate([got, kept], 1)
+    )
+    wide = wide_direction(wide)
+    low_wide = to_low(wide)
+    other_wide = swap_cores(low_wide)
+    direct_up = jnp.where(first_core, low_wide, other_wide).astype(jnp.float32)
+    direct_down = jnp.where(first_core, other_wide, low_wide)
+    direct_down = (
+        jnp.concatenate(
+            [direct_down[:, :half_down], direct_down[:, half_up : half_up + half_down]], 1
+        )
+        .astype(jnp.float32)
+        .T
+    )
+    low_sq = to_low(square_directions(sum_sq + 0.95 * sq_moment_new))
+    other_sq = swap_cores(low_sq)
+    direct_sq = jnp.where(
+        first_core,
+        jnp.concatenate([low_sq, other_sq], 0),
+        jnp.concatenate([other_sq, low_sq], 0),
+    ).astype(jnp.float32)
+    directions = (direct_sq, direct_up, direct_down)
     shrink = 1.0 - MUON_RATE * DECAY
     square_new = motion_squares * shrink - MUON_RATE * 0.2 * math.sqrt(WIDTH) * directions[0]
     up_new = (

time: 1260 us -> 802 us (0.64)
  waiting for transfers between devices: 499 us -> 120 us
  loops' own time: 123 us -> 0 us
  blocking collectives: 80.1 us -> 0 us
  Pallas kernels: 0 us -> 51.2 us
  local copies, waits for them, and re-layouts: 167 us -> 205 us
  other arithmetic: 87.7 us -> 118 us
  starting transfers between devices: 18.3 us -> 43.9 us
  matrix products: 257 us -> 242 us
    psum x2 -> x0, waiting for transfers between devices: 442 us -> none  [the longest x1 247 us: shards(): lax.psum((jnp.stack(results[:10]), results[10], results[11]), 'frames')]
    another operation x12 -> x0, loops' own time: 123 us -> none  [shards(): lax.cond(frame_index == owner_id, orthogonalize, jnp.zeros_like, matrix)]
    ppermute x0 -> x22, waiting for transfers between devices: none -> 96.7 us  [the longest x16 96.7 us: swap_frames(): return lax.ppermute(values, 'frames', [(i, i ^ bit) for i in range(size)])]
    psum x1 -> x0, blocking collectives: 80.1 us -> none  [shards(): lax.psum(jnp.sum(frame_valid * jnp.square(residual)), ('frames', 'dp'))]
    pallas_call x0 -> x2, Pallas kernels: none -> 51.2 us  [the longest x1 35.1 us: square_directions(): pl.pallas_call(square_directions_kernel, out_shape=jax.ShapeDtypeStruct(m...]
    ppermute x0 -> x22, starting transfers between devices: none -> 25.2 us  [the longest x16 23.2 us: swap_frames(): return lax.ppermute(values, 'frames', [(i, i ^ bit) for i in range(size)])]
    reshape x0 -> x14, local copies, waits for them, and re-layouts: none -> 22 us  [the longest x2 6 us: half_of(): lax.dynamic_slice_in_dim(grad_sq, core * half_sq, half_sq, 0)]
    all_to_all x3, waiting for transfers between devices: 42.8 us -> 23.2 us  [the longest x2 13.7 us: to_positions(): lax.all_to_all(jnp.swapaxes(values, 0, 1), ('frames', 'dp'), split_axis=0...]
  transfers between devices with their start and end apart: 8 -> 25, of which waited for: 8 -> 15; matrix products, arithmetic and copies ran while one was open for 2% -> 8% of each run, Pallas kernels for 0% -> 6%
where the time goes in v1:
time: 802 us; the launch traced here: 789 us
  matrix products  242 us (30%)
  local copies, waits for them, and re-layouts  205 us (26%)
  waiting for transfers between devices  120 us (15%)
  other arithmetic  118 us (15%)
  Pallas kernels  51.2 us (6%)
  starting transfers between devices  43.9 us (5%)
  between operations  9.48 us (1%)
    ppermute x16, waiting for transfers between devices, swap_frames(): return lax.ppermute(values, 'frames', [(i, i ^ bit) for i in range(size)])  96.7 us
    convert_element_type x29, local copies, waits for them, and re-layouts, to_low(): return values.astype(jnp.bfloat16)  68.7 us
    dot_general x25, matrix products, product(): jnp.einsum('...i,ij->...j', left, right, preferred_element_type=jnp.float32)  62.4 us
    conv_general_dilated x5, matrix products, convolve(): lax.conv_general_dilated(images, kernel, (1, 1), 'SAME', dimension_number...  50.4 us
    unnamed x251, local copies, waits for them, and re-layouts  46.8 us
    dot_general x12, matrix products, product_back(): jnp.einsum('...j,ij->...i', left, right, preferred_element_type=jnp.float32)  35.8 us
    pallas_call x1, Pallas kernels, square_directions(): pl.pallas_call(square_directions_kernel, out_shape=jax.ShapeDtypeStruct(m...  35.1 us
    another operation x8, local copies, waits for them, and re-layouts  28.7 us
  transfers between devices with their start and end apart: 25, of which 15 were waited for; matrix products, arithmetic and copies ran while one was open for 8% of the time, Pallas kernels for 6%

profile of v1, /device:TPU:0, one launch (start us, length us, event | category | flops | bytes accessed | tf_op | source)
XLA Modules:
  0.0 789.0 jit_solution(15858800649852933033)
XLA Ops:
  30.8 13.6 %fusion.39 = f32[1,32,32,320]{3,0,2,1:T(1,128)S(1)} fusion(bf16[2,3,3,320,320]{4,3,2,1,0:T(8,128)(2,1)S(1)} %copy-done.109, bf16[1,32,32,320]{3,2,1,0:T(8,128)(2,1)S(1)} %multiply_convert_fusion.10), kind=kOutput, calls=%fused_computation.92 | convolution fusion | flops 1809612800 | bytes 4308992 | tf_op jit(solution)/shard_map/conv_general_dilated | solution.py:45
  47.5 15.4 %fusion.40 = f32[1,32,32,320]{3,0,2,1:T(1,128)S(1)} fusion(bf16[2,3,3,320,320]{4,3,2,1,0:T(8,128)(2,1)} %param.37, bf16[1,32,32,320]{3,2,1,0:T(8,128)(2,1)S(1)} %multiply_convert_fusion.9), kind=kOutput, calls=%fused_computation.93 | convolution fusion | flops 1809612800 | bytes 4177920 | tf_op jit(solution)/shard_map/conv_general_dilated | solution.py:45
  75.3 17.7 %fusion.256 = (f32[8,1024]{1,0:T(8,128)S(1)}, f32[8,1024,1024]{1,2,0:T(8,128)}) fusion(bf16[1024,8,40]{0,2,1:T(8,128)(2,1)} %bitcast.426, bf16[1024,8,40]{0,2,1:T(8,128)(2,1)} %bitcast.427), kind=kOutput, calls=%fused_computation.517 | convolution fusion | flops 696255488 | bytes 34897920 | tf_op jit(solution)/shard_map/sub | solution.py:89
  93.0 12.4 %fusion.73 = bf16[8,40,1024]{2,1,0:T(8,128)(2,1)S(1)} fusion(bf16[1024,8,40]{0,2,1:T(8,128)(2,1)S(1)} %bitcast.425, f32[8,1024,1024]{1,2,0:T(8,128)} %get-tuple-element.121, f32[8,1024]{1,0:T(8,128)S(1)} %get-tuple-element.120), kind=kOutput, calls=%fused_computation.198 | convolution fusion | flops 688193536 | bytes 34897920 | tf_op jit(solution)/shard_map/hqk,khd->qhd/dot_general | solution.py:90
  121.0 7.1 fusion.114
  128.2 16.6 %fusion.260 = (f32[320]{0:T(512)S(1)}, f32[1024,320]{0,1:T(8,128)S(1)}) fusion(f32[320]{0:T(512)S(1)} %get-tuple-element.32, bf16[8,320,320]{2,1,0:T(8,128)(2,1)} %param.42, f32[1024,320]{0,1:T(8,128)S(1)} %get-tuple-element.127, bf16[1280,320]{0,1:T(8,128)(2,1)} %param.45, f32[1024,2560]{1,0:T(8,128)} %fusion.114, f32[320]{0:T(512)S(1)} %get-tuple-element.33, ...), kind=kOutput, calls=%fused_computation.521 | convolution fusion | flops 1138032384 | bytes 16800000 | tf_op jit(solution)/shard_map/...i,ij->...j/dot_general | solution.py:35
  149.9 9.4 %all-to-all-start = ((bf16[16,2,10240]{2,1,0:T(2,128)(2,1)}), bf16[16,2,10240]{2,1,0:T(2,128)(2,1)S(1)}, u32[]{:S(2)}, u32[]{:S(2)}) async-start(bf16[16,2,10240]{2,1,0:T(2,128)(2,1)} %reshape.1865), calls=%async_computation | async-start | bytes 1310720 | tf_op jit(solution)/shard_map/all_to_all | solution.py:574
  197.2 6.3 fusion.264
  240.0 6.3 fusion.266
  262.9 12.7 %fusion.31 = (bf16[64,16,1280]{2,1,0:T(8,128)(2,1)S(1)}, f32[64,1,16,1280]{3,2,0,1:T(8,128)}) fusion(f32[64,1,16,2560]{3,2,0,1:T(8,128)S(1)} %convolution_bitcast_fusion), kind=kLoop, calls=%fused_computation.77 | loop fusion | flops 86507520 | bytes 18350080 | tf_op jit(solution)/shard_map/reshape.71
  287.2 9.5 %all-to-all-done.1 = bf16[64,16,320]{2,0,1:T(8,128)(2,1)} async-done(((bf16[64,16,320]{2,0,1:T(8,128)(2,1)}), bf16[64,16,320]{2,0,1:T(8,128)(2,1)}, u32[]{:S(2)}, u32[]{:S(2)}) %all-to-all-start.1) | async-done | bytes 655392 | tf_op jit(solution)/shard_map/all_to_all | solution.py:592
  306.2 11.2 %fusion.59 = f32[1,32,32,4]{3,0,2,1:T(1,128)} fusion(bf16[3,3,320,4]{2,3,1,0:T(4,128)(2,1)S(1)} %copy-done.110, bf16[1,32,32,320]{3,2,1,0:T(8,128)(2,1)S(1)} %multiply_convert_fusion.7), kind=kOutput, calls=%fused_computation.166 | convolution fusion | flops 22620160 | bytes 694784 | tf_op jit(solution)/shard_map/conv_general_dilated | solution.py:45
  351.5 9.4 %all-to-all-done.2 = bf16[16,2,10240]{2,1,0:T(2,128)(2,1)} async-done(((bf16[16,2,10240]{2,1,0:T(2,128)(2,1)}), bf16[16,2,10240]{2,1,0:T(2,128)(2,1)}, u32[]{:S(2)}, u32[]{:S(2)}) %all-to-all-start.2) | async-done | bytes 655392 | tf_op jit(solution)/shard_map/all_to_all | solution.py:574
  367.8 7.8 multiply_add_fusion
  525.6 7.6 pad_maximum_fusion
  542.3 6.7 fusion.28
  555.0 24.6 %collective-permute-done.3 = f32[2240,128]{1,0:T(8,128)} collective-permute-done((f32[2240,128]{1,0:T(8,128)}, f32[2240,128]{1,0:T(8,128)}, u32[]{:S(2)}, u32[]{:S(2)}) %collective-permute-start.3) | collective-permute-done | bytes 1146912 | tf_op jit(solution)/shard_map/ppermute | solution.py:438
  585.3 10.6 %collective-permute-done.4 = f32[1120,128]{1,0:T(8,128)S(1)} collective-permute-done((f32[1120,128]{1,0:T(8,128)S(1)}, f32[1120,128]{1,0:T(8,128)S(1)}, u32[]{:S(2)}, u32[]{:S(2)}) %collective-permute-start.4) | collective-permute-done | bytes 573472 | tf_op jit(solution)/shard_map/ppermute | solution.py:438
  598.4 5.1 collective-permute-done.5
  633.4 5.9 collective-permute-done.16
  643.4 13.7 %collective-permute-done.17 = f32[1120,128]{1,0:T(8,128)} collective-permute-done((f32[1120,128]{1,0:T(8,128)S(1)}, f32[1120,128]{1,0:T(8,128)}, u32[]{:S(2)}, u32[]{:S(2)}) %collective-permute-start.17) | collective-permute-done | bytes 573472 | tf_op jit(solution)/shard_map/ppermute | solution.py:438
  659.5 19.6 %collective-permute-done.10 = f32[2240,128]{1,0:T(8,128)} collective-permute-done((f32[2240,128]{1,0:T(8,128)S(1)}, f32[2240,128]{1,0:T(8,128)}, u32[]{:S(2)}, u32[]{:S(2)}) %collective-permute-start.10) | collective-permute-done | bytes 1146912 | tf_op jit(solution)/shard_map/ppermute | solution.py:438
  706.8 35.1 %square_directions.1 = f32[5,320,320]{2,1,0:T(8,128)} custom-call(f32[5,320,320]{2,1,0:T(8,128)} %get-tuple-element.74.x_ref), custom_call_target="tpu_custom_call" | custom-call | tf_op jit(solution)/shard_map/square_directions/pallas_call | solution.py:386
  748.5 16.1 %wide_direction.1 = f32[320,2560]{1,0:T(8,128)} custom-call(f32[320,2560]{1,0:T(8,128)} %maximum_select_fusion.x_ref), custom_call_target="tpu_custom_call" | custom-call | tf_op jit(solution)/shard_map/wide_direction/pallas_call | solution.py:418
  (629 shorter events, 479.1 us)
Async XLA Ops:
  4.0 8.8 %collective-permute-start = (bf16[78,768]{1,0:T(8,128)(2,1)}, bf16[78,768]{1,0:T(8,128)(2,1)}, u32[]{:S(2)}, u32[]{:S(2)}) collective-permute-start(bf16[78,768]{1,0:T(8,128)(2,1)} %pad_maximum_fusion.3), channel_id=1, source_target_pairs={{0,1},{1,0},{2,3},{3,2},{4,5},{5,4},{6,7},{7,6},{8,9},{9,8},{10,11... | collective-permute-start | bytes 359432 | tf_op jit(solution)/shard_map/ppermute | solution.py:429
  149.9 20.1 %all-to-all-start = ((bf16[16,2,10240]{2,1,0:T(2,128)(2,1)}), bf16[16,2,10240]{2,1,0:T(2,128)(2,1)S(1)}, u32[]{:S(2)}, u32[]{:S(2)}) async-start(bf16[16,2,10240]{2,1,0:T(2,128)(2,1)} %reshape.1865), calls=%async_computation | async-start | bytes 1310720 | tf_op jit(solution)/shard_map/all_to_all | solution.py:574
  280.2 16.5 %all-to-all-start.1 = ((bf16[64,16,320]{2,0,1:T(8,128)(2,1)}), bf16[64,16,320]{2,0,1:T(8,128)(2,1)}, u32[]{:S(2)}, u32[]{:S(2)}) async-start(bf16[64,16,320]{2,0,1:T(8,128)(2,1)} %copy.317), calls=%async_computation.1 | async-start | bytes 1572864 | tf_op jit(solution)/shard_map/all_to_all | solution.py:592
  345.4 15.4 %all-to-all-start.2 = ((bf16[16,2,10240]{2,1,0:T(2,128)(2,1)}), bf16[16,2,10240]{2,1,0:T(2,128)(2,1)}, u32[]{:S(2)}, u32[]{:S(2)}) async-start(bf16[16,2,10240]{2,1,0:T(2,128)(2,1)} %reshape.1867), calls=%async_computation.2 | async-start | bytes 1310720 | tf_op jit(solution)/shard_map/all_to_all | solution.py:574
  533.2 9.1 %collective-permute-start.2 = (f32[8864,128]{1,0:T(8,128)}, f32[8864,128]{1,0:T(8,128)}, u32[]{:S(2)}, u32[]{:S(2)}) collective-permute-start(f32[8864,128]{1,0:T(8,128)} %pad_maximum_fusion), channel_id=1, source_target_pairs={{0,1},{1,0},{2,3},{3,2},{4,5},{5,4},{6,7},{7,6},{8,9},{9,8},{10,11... | collective-permute-start | bytes 13615112 | tf_op jit(solution)/shard_map/ppermute | solution.py:429
  551.8 27.8 %collective-permute-start.3 = (f32[2240,128]{1,0:T(8,128)}, f32[2240,128]{1,0:T(8,128)}, u32[]{:S(2)}, u32[]{:S(2)}) collective-permute-start(f32[2240,128]{1,0:T(8,128)} %constant_dynamic-slice_fusion.7), channel_id=1, source_target_pairs={{0,4},{2,6},{4,0},{6,2},{8,12},{10,14},{12,8},{14,10},{16,20},{18,... | collective-permute-start | bytes 3440648 | tf_op jit(solution)/shard_map/ppermute | solution.py:438
  554.4 28.3 %collective-permute-start.11 = (f32[2240,128]{1,0:T(8,128)}, f32[2240,128]{1,0:T(8,128)}, u32[]{:S(2)}, u32[]{:S(2)}) collective-permute-start(f32[2240,128]{1,0:T(8,128)} %constant_dynamic-slice_fusion.3), channel_id=1, source_target_pairs={{0,2},{2,0},{4,6},{6,4},{8,10},{10,8},{12,14},{14,12},{16,18},{18,... | collective-permute-start | bytes 3440648 | tf_op jit(solution)/shard_map/ppermute | solution.py:438
  581.4 14.5 %collective-permute-start.4 = (f32[1120,128]{1,0:T(8,128)S(1)}, f32[1120,128]{1,0:T(8,128)S(1)}, u32[]{:S(2)}, u32[]{:S(2)}) collective-permute-start(f32[1120,128]{1,0:T(8,128)S(1)} %constant_dynamic-slice_fusion.6), channel_id=1, source_target_pairs={{0,2},{2,0},{4,6},{6,4},{8,10},{10,8},{12,14},{14,12},{16,18},{18,... | collective-permute-start | bytes 1720328 | tf_op jit(solution)/shard_map/ppermute | solution.py:438
  584.2 14.1 %collective-permute-start.12 = (f32[1120,128]{1,0:T(8,128)S(1)}, f32[1120,128]{1,0:T(8,128)S(1)}, u32[]{:S(2)}, u32[]{:S(2)}) collective-permute-start(f32[1120,128]{1,0:T(8,128)S(1)} %constant_dynamic-slice_fusion.2), channel_id=1, source_target_pairs={{0,4},{2,6},{4,0},{6,2},{8,12},{10,14},{12,8},{14,10},{16,20},{18,... | collective-permute-start | bytes 1720328 | tf_op jit(solution)/shard_map/ppermute | solution.py:438
  596.0 7.5 collective-permute-start.5
  603.5 6.3 collective-permute-start.6
  604.9 12.5 %collective-permute-start.13 = (f32[560,128]{1,0:T(8,128)S(1)}, f32[560,128]{1,0:T(8,128)S(1)}, u32[]{:S(2)}, u32[]{:S(2)}) collective-permute-start(f32[560,128]{1,0:T(8,128)S(1)} %constant_dynamic-slice_fusion.1), channel_id=1, source_target_pairs={{0,8},{2,10},{4,12},{6,14},{8,0},{10,2},{12,4},{14,6},{16,24},{18,... | collective-permute-start | bytes 860168 | tf_op jit(solution)/shard_map/ppermute | solution.py:438
  609.9 7.8 collective-permute-start.7
  617.4 7.2 collective-permute-start.14
  617.7 11.6 %collective-permute-start.8 = (f32[560,128]{1,0:T(8,128)S(1)}, f32[560,128]{1,0:T(8,128)S(1)}, u32[]{:S(2)}, u32[]{:S(2)}) collective-permute-start(f32[560,128]{1,0:T(8,128)S(1)} %maximum_select_fusion.8), channel_id=1, source_target_pairs={{0,8},{2,10},{4,12},{6,14},{8,0},{10,2},{12,4},{14,6},{16,24},{18,... | collective-permute-start | bytes 860168 | tf_op jit(solution)/shard_map/ppermute | solution.py:438
  624.7 7.9 %collective-permute-start.15 = (f32[280,128]{1,0:T(8,128)S(1)}, f32[280,128]{1,0:T(8,128)S(1)}, u32[]{:S(2)}, u32[]{:S(2)}) collective-permute-start(f32[280,128]{1,0:T(8,128)S(1)} %dynamic-slice_add_fusion.6), channel_id=1, source_target_pairs={{0,16},{2,18},{4,20},{6,22},{8,24},{10,26},{12,28},{14,30},{16,0},... | collective-permute-start | bytes 430088 | tf_op jit(solution)/shard_map/ppermute | solution.py:438
  629.4 13.8 %collective-permute-start.9 = (f32[1120,128]{1,0:T(8,128)S(1)}, f32[1120,128]{1,0:T(8,128)S(1)}, u32[]{:S(2)}, u32[]{:S(2)}) collective-permute-start(f32[1120,128]{1,0:T(8,128)S(1)} %maximum_select_fusion.6), channel_id=1, source_target_pairs={{0,2},{2,0},{4,6},{6,4},{8,10},{10,8},{12,14},{14,12},{16,18},{18,... | collective-permute-start | bytes 1720328 | tf_op jit(solution)/shard_map/ppermute | solution.py:438
  632.6 6.7 collective-permute-start.16
  639.3 17.8 %collective-permute-start.17 = (f32[1120,128]{1,0:T(8,128)S(1)}, f32[1120,128]{1,0:T(8,128)}, u32[]{:S(2)}, u32[]{:S(2)}) collective-permute-start(f32[1120,128]{1,0:T(8,128)S(1)} %maximum_select_fusion.7), channel_id=1, source_target_pairs={{0,4},{2,6},{4,0},{6,2},{8,12},{10,14},{12,8},{14,10},{16,20},{18,... | collective-permute-start | bytes 1720328 | tf_op jit(solution)/shard_map/ppermute | solution.py:438
  643.3 35.8 %collective-permute-start.10 = (f32[2240,128]{1,0:T(8,128)S(1)}, f32[2240,128]{1,0:T(8,128)}, u32[]{:S(2)}, u32[]{:S(2)}) collective-permute-start(f32[2240,128]{1,0:T(8,128)S(1)} %maximum_select_fusion.4), channel_id=1, source_target_pairs={{0,4},{2,6},{4,0},{6,2},{8,12},{10,14},{12,8},{14,10},{16,20},{18,... | collective-permute-start | bytes 3440648 | tf_op jit(solution)/shard_map/ppermute | solution.py:438
  659.5 26.0 %collective-permute-start.18 = (f32[2240,128]{1,0:T(8,128)}, f32[2240,128]{1,0:T(8,128)}, u32[]{:S(2)}, u32[]{:S(2)}) collective-permute-start(f32[2240,128]{1,0:T(8,128)} %maximum_select_fusion.5), channel_id=1, source_target_pairs={{0,2},{2,0},{4,6},{6,4},{8,10},{10,8},{12,14},{14,12},{16,18},{18,... | collective-permute-start | bytes 3440648 | tf_op jit(solution)/shard_map/ppermute | solution.py:438
  698.4 46.1 %collective-permute-start.20 = (f32[320,1280]{1,0:T(8,128)}, f32[320,1280]{1,0:T(8,128)}, u32[]{:S(2)}, u32[]{:S(2)}) collective-permute-start(f32[320,1280]{1,0:T(8,128)} %pad_select_fusion), channel_id=1, source_target_pairs={{0,1},{1,0},{2,3},{3,2},{4,5},{5,4},{6,7},{7,6},{8,9},{9,8},{10,11... | collective-permute-start | bytes 4915208 | tf_op jit(solution)/shard_map/ppermute | solution.py:429
  743.9 26.3 %collective-permute-start.19 = (bf16[5,320,320]{2,1,0:T(8,128)(2,1)S(1)}, bf16[5,320,320]{2,1,0:T(8,128)(2,1)}, u32[]{:S(2)}, u32[]{:S(2)}) collective-permute-start(bf16[5,320,320]{2,1,0:T(8,128)(2,1)S(1)} %convert_element_type.675), channel_id=1, source_target_pairs={{0,1},{1,0},{2,3},{3,2},{4,5},{5,4},{6,7},{7,6},{8,9},{9,8},{10,11... | collective-permute-start | bytes 3072008 | tf_op jit(solution)/shard_map/ppermute | solution.py:429
  767.9 9.7 %collective-permute-start.21 = (bf16[320,2560]{1,0:T(8,128)(2,1)}, bf16[320,2560]{1,0:T(8,128)(2,1)}, u32[]{:S(2)}, u32[]{:S(2)}) collective-permute-start(bf16[320,2560]{1,0:T(8,128)(2,1)} %convert_element_type.677), channel_id=1, source_target_pairs={{0,1},{1,0},{2,3},{3,2},{4,5},{5,4},{6,7},{7,6},{8,9},{9,8},{10,11... | collective-permute-start | bytes 4915208 | tf_op jit(solution)/shard_map/ppermute | solution.py:429
  (121 other events, 549.9 us)

commit v2 on v0

v2 whole, which is shorter than its diff:
```python
import math

import jax
import jax.numpy as jnp
import numpy as np
from jax import lax
from jax.experimental import pallas as pl
from jax.experimental.pallas import tpu as pltpu
from jax.sharding import PartitionSpec as P

WIDTH = 320
HEADS = 8
HEAD_DIM = 40
FF_INNER = 1280
CLIP = 16
HALF = 8
PIX = 1024
LATENT = 32
TEXT_LEN = 77
TEXT_DIM = 768
GN_GROUPS = 32
F32 = jnp.float32
BF16 = jnp.bfloat16
VMEM_LIMIT = 60 * 2**20
OWN = PIX // CLIP
SLOT = 64
SLOTS = HEADS * SLOT
CHUNK = 256
CHUNKS = PIX // CHUNK
GROUP = 128
SCALE = 1.0 / math.sqrt(HEAD_DIM)


def to_low(values):
    return values.astype(BF16)


def dot(left, right):
    return lax.dot_general(left, right, (((1,), (0,)), ((), ())), preferred_element_type=F32)


def dot_nt(left, right):
    return lax.dot_general(left, right, (((1,), (1,)), ((), ())), preferred_element_type=F32)


def dot_tn(left, right):
    return lax.dot_general(left, right, (((0,), (0,)), ((), ())), preferred_element_type=F32)


def in_vmem():
    return pl.BlockSpec(memory_space=pltpu.VMEM)


def in_smem():
    return pl.BlockSpec(memory_space=pltpu.SMEM)


def whole(shape):
    return pl.BlockSpec(shape, lambda *_: (0,) * len(shape))


def rows_of(width):
    return pl.BlockSpec((CHUNK, width), lambda c: (c, 0))


def slot_selector():
    out = np.zeros((WIDTH, SLOTS), np.float32)
    for head in range(HEADS):
        for j in range(HEAD_DIM):
            out[head * HEAD_DIM + j, head * SLOT + j] = 1.0
    return jnp.asarray(out, BF16)


def frame_codes():
    positions = np.arange(CLIP, dtype=np.float32)[:, None]
    column = np.arange(WIDTH)
    frequency = np.exp(np.float32(-math.log(10000.0)) * (2 * (column // 2)).astype(np.float32) / WIDTH)
    angles = positions * frequency.astype(np.float32)
    codes = np.where(column % 2 == 0, np.sin(angles), np.cos(angles)).astype(np.float32)
    return jnp.asarray(np.tile(np.repeat(codes, 8, axis=0), (CHUNK // GROUP, 1)))


def unpack_positions(packed_ref, wide_ref):
    wide_ref[:, :, 0:128] = packed_ref[:, 0:64, :].astype(F32)
    wide_ref[:, :, 128:256] = packed_ref[:, 64:128, :].astype(F32)
    last = packed_ref[:, 128:160, :].astype(F32)
    wide_ref[:, 0:32, 256:320] = last[:, :, 0:64]
    wide_ref[:, 32:64, 256:320] = last[:, :, 64:128]


def pack_positions(wide_ref, packed_ref):
    packed_ref[:, 0:64, :] = to_low(wide_ref[:, :, 0:128])
    packed_ref[:, 64:128, :] = to_low(wide_ref[:, :, 128:256])
    last = jnp.concatenate([wide_ref[:, 0:32, 256:320], wide_ref[:, 32:64, 256:320]], axis=2)
    packed_ref[:, 128:160, :] = to_low(last)


def chunk_tokens(wide_ref, step):
    parts = []
    for group in range(CHUNK // GROUP):
        start = pl.multiple_of(step * (CHUNK // CLIP) + 8 * group, 8)
        parts.append(wide_ref[:, pl.ds(start, 8), :].reshape(GROUP, WIDTH))
    return jnp.concatenate(parts, axis=0)


def put_chunk_tokens(wide_ref, step, tokens):
    for group in range(CHUNK // GROUP):
        start = pl.multiple_of(step * (CHUNK // CLIP) + 8 * group, 8)
        part = tokens[group * GROUP : (group + 1) * GROUP].reshape(CLIP, 8, WIDTH)
        wide_ref[:, pl.ds(start, 8), :] = part


def normal_parts(values):
    centre = jnp.mean(values, axis=-1, keepdims=True)
    shifted = values - centre
    scale = lax.rsqrt(jnp.mean(shifted * shifted, axis=-1, keepdims=True) + 1e-05)
    return shifted * scale, scale


def normal_back(grad, normal, scale, gain):
    inner = grad * gain
    return scale * (
        inner
        - jnp.mean(inner, axis=-1, keepdims=True)
        - normal * jnp.mean(inner * normal, axis=-1, keepdims=True)
    )


def erf_parts(gate):
    bell = jnp.exp(-0.5 * gate * gate)
    size = jnp.abs(gate) * (1.0 / math.sqrt(2.0))
    t = 1.0 / (1.0 + 0.3275911 * size)
    poly = t * (
        0.254829592
        + t * (-0.284496736 + t * (1.421413741 + t * (-1.453152027 + t * 1.061405429)))
    )
    tail = poly * bell
    return jnp.where(gate < 0.0, tail - 1.0, 1.0 - tail), bell


def gelu_parts(gate):
    erf, bell = erf_parts(gate)
    share = 0.5 + 0.5 * erf
    return gate * share, share + gate * bell * (1.0 / math.sqrt(2.0 * math.pi))


def lane_halves(values):
    lane = lax.broadcasted_iota(jnp.int32, values.shape, 1)
    zero = jnp.zeros_like(values)
    return jnp.concatenate(
        [jnp.where(lane < SLOT, values, zero), jnp.where(lane < SLOT, zero, values)], axis=0
    )


def key_bias(count, queries_first):
    shape = (GROUP, 2 * GROUP) if queries_first else (2 * GROUP, GROUP)
    row = lax.broadcasted_iota(jnp.int32, shape, 0)
    column = lax.broadcasted_iota(jnp.int32, shape, 1)
    key = (column if queries_first else row) % GROUP
    valid = (row % 8 == column % 8) & (key // 8 < count)
    return jnp.where(valid, 0.0, -1e30).astype(F32)


def attend_chunk(qkv, bias):
    out = []
    for group in range(CHUNK // GROUP):
        rows = slice(group * GROUP, (group + 1) * GROUP)
        pairs = []
        for pair in range(HEADS // 2):
            lanes = pair * 2 * SLOT
            queries = qkv[rows, lanes : lanes + GROUP]
            keys = lane_halves(qkv[rows, SLOTS + lanes : SLOTS + lanes + GROUP])
            values = lane_halves(qkv[rows, 2 * SLOTS + lanes : 2 * SLOTS + lanes + GROUP])
            scores = dot_nt(queries, keys) * SCALE + bias
            probs = []
            for part in (scores[:, :GROUP], scores[:, GROUP:]):
                raised = jnp.exp(part - jnp.max(part, axis=1, keepdims=True))
                probs.append(raised * (1.0 / jnp.sum(raised, axis=1, keepdims=True)))
            pairs.append(to_low(dot(to_low(jnp.concatenate(probs, axis=1)), values)))
        out.append(jnp.concatenate(pairs, axis=1))
    return jnp.concatenate(out, axis=0)


def motion_forward_kernel(
    count_ref, keep_ref, arrived_ref, codes_ref, vec_ref, w_in_ref, w_qkv_ref, w_o_ref, w_up_ref, w_down_ref, w_out_ref,
    branch_ref, u_ref, u2_ref, u3_ref, qkv1_ref, qkv2_ref, o1_ref, o2_ref, last_ref,
    wide, back,
):
    step = pl.program_id(0)

    @pl.when(step == 0)
    def _():
        unpack_positions(arrived_ref, wide)

    def vec(i):
        return vec_ref[i : i + 1, :]

    bias = key_bias(count_ref[0], True)
    normed = chunk_tokens(wide, step)
    inputs = to_low(normed * vec(0) + vec(1))
    stream = dot(inputs, w_in_ref[...]) + vec(2)
    for index, (first, x_ref, qkv_ref, o_ref) in enumerate(((3, u_ref, qkv1_ref, o1_ref), (6, u2_ref, qkv2_ref, o2_ref))):
        x_ref[...] = stream
        normal = normal_parts(stream)[0]
        a = to_low(normal * vec(first) + vec(first + 1) + codes_ref[...])
        qkv = to_low(dot(a, w_qkv_ref[index]))
        qkv_ref[...] = qkv
        mixture = attend_chunk(qkv, bias)
        o_ref[...] = mixture
        stream = stream + (dot(mixture, w_o_ref[index]) + vec(first + 2))
    u3_ref[...] = stream
    c = to_low(normal_parts(stream)[0] * vec(9) + vec(10))
    gate_up = dot(c, w_up_ref[...])
    inner = to_low(gate_up[:, :FF_INNER] * gelu_parts(gate_up[:, FF_INNER:])[0])
    last = to_low(stream + (dot(inner, w_down_ref[...]) + vec(11)))
    last_ref[...] = last
    put_chunk_tokens(back, step, (dot(last, w_out_ref[...]) + vec(12)) * keep_ref[0])

    @pl.when(step == CHUNKS - 1)
    def _():
        pack_positions(back, branch_ref)


def motion_forward(arrived, count, keep, weights, vectors):
    outs = [
        ((CLIP, 160, 128), BF16, None),
        ((PIX, WIDTH), F32, WIDTH), ((PIX, WIDTH), F32, WIDTH), ((PIX, WIDTH), F32, WIDTH),
        ((PIX, 3 * SLOTS), BF16, 3 * SLOTS), ((PIX, 3 * SLOTS), BF16, 3 * SLOTS),
        ((PIX, SLOTS), BF16, SLOTS), ((PIX, SLOTS), BF16, SLOTS),
        ((PIX, WIDTH), BF16, WIDTH),
    ]
    operands = (arrived, frame_codes(), vectors, weights["in"], weights["qkv"], weights["o"], weights["up"], weights["down"], weights["out"])
    return pl.pallas_call(
        motion_forward_kernel,
        grid=(CHUNKS,),
        in_specs=[in_smem(), in_smem()] + [whole(x.shape) for x in operands],
        out_specs=[whole(s) if w is None else rows_of(w) for s, _, w in outs],
        out_shape=[jax.ShapeDtypeStruct(s, d) for s, d, _ in outs],
        scratch_shapes=[pltpu.VMEM((CLIP, OWN, WIDTH), F32), pltpu.VMEM((CLIP, OWN, WIDTH), F32)],
        compiler_params=pltpu.CompilerParams(vmem_limit_bytes=VMEM_LIMIT),
        name="motion_forward",
    )(count, keep, *operands)


def prepare_kernel(sq_ref, up_ref, down_ref, sel_ref, w_in, w_qkv, w_o, w_up, w_down, w_out, t_in, t_qkv, t_o, t_up, t_down, t_out):
    sel = sel_ref[...]
    low = [to_low(sq_ref[i]) for i in range(10)]
    w_in[...] = low[0]
    t_in[...] = low[0].T
    w_out[...] = low[9]
    t_out[...] = low[9].T
    for index, first in enumerate((1, 5)):
        for j in range(3):
            padded = to_low(dot(low[first + j], sel))
            w_qkv[index, :, j * SLOTS : (j + 1) * SLOTS] = padded
            t_qkv[index, j * SLOTS : (j + 1) * SLOTS, :] = padded.T
        padded = to_low(dot_nt(low[first + 3].T, sel.T))
        t_o[index] = padded
        w_o[index] = padded.T
    up = to_low(up_ref[...])
    w_up[...] = up
    t_up[...] = up.T
    down = to_low(down_ref[...])
    w_down[...] = down
    t_down[...] = down.T


def prepare(squares, up, down):
    shapes = {
        "in": (WIDTH, WIDTH), "qkv": (2, WIDTH, 3 * SLOTS), "o": (2, SLOTS, WIDTH), "up": (WIDTH, 2 * FF_INNER),
        "down": (FF_INNER, WIDTH), "out": (WIDTH, WIDTH),
        "in_t": (WIDTH, WIDTH), "qkv_t": (2, 3 * SLOTS, WIDTH), "o_t": (2, WIDTH, SLOTS), "up_t": (2 * FF_INNER, WIDTH),
        "down_t": (WIDTH, FF_INNER), "out_t": (WIDTH, WIDTH),
    }
    made = pl.pallas_call(
        prepare_kernel,
        in_specs=[in_vmem()] * 4,
        out_specs=[in_vmem()] * len(shapes),
        out_shape=[jax.ShapeDtypeStruct(s, BF16) for s in shapes.values()],
        compiler_params=pltpu.CompilerParams(vmem_limit_bytes=VMEM_LIMIT),
        name="motion_weights",
    )(squares, up, down, slot_selector())
    return dict(zip(shapes, made))


def add_to(ref, step, value):
    @pl.when(step == 0)
    def _():
        ref[...] = value

    @pl.when(step > 0)
    def _():
        ref[...] += value


def column_sum(values):
    return jnp.sum(values, axis=0, keepdims=True)


def feed_backward_kernel(
    keep_ref, grad_ref, u3_ref, last_ref, vec_ref, w_up_ref, t_up_ref, t_down_ref, t_out_ref,
    du3_ref, g_wide_ref, g_out_ref, g_vec_ref,
    wide,
):
    step = pl.program_id(0)

    @pl.when(step == 0)
    def _():
        unpack_positions(grad_ref, wide)
        g_wide_ref[...] = jnp.zeros_like(g_wide_ref)

    gain = vec_ref[9:10, :]
    dbranch = to_low(chunk_tokens(wide, step) * keep_ref[0])
    add_to(g_out_ref, step, dot_tn(last_ref[...], dbranch))
    du4 = dot(dbranch, t_out_ref[...])
    d4 = to_low(du4)
    normal, scale = normal_parts(u3_ref[...])
    c = to_low(normal * gain + vec_ref[10:11, :])
    z = dot(c, w_up_ref[...])
    value = z[:, :FF_INNER]
    gelu, slope = gelu_parts(z[:, FF_INNER:])
    inner = to_low(value * gelu)
    dinner = dot(d4, t_down_ref[...])
    dz = to_low(jnp.concatenate([dinner * gelu, dinner * value * slope], axis=1))
    g_down = dot_tn(d4, inner)
    g_up = dot_tn(c, dz)
    for half in range(2):
        for tile in range(10):
            start = half * FF_INNER + tile * 128
            g_wide_ref[half, tile_rows(tile)] += g_up[:, start : start + 128]
        for tile in range(5):
            start = half * (FF_INNER // 2) + tile * 128
            g_wide_ref[half, tile_rows(10 + tile)] += g_down[:, start : start + 128]
    dc = dot(dz, t_up_ref[...])
    du3_ref[...] = du4 + normal_back(dc, normal, scale, gain)
    rows = [column_sum(dc * normal), column_sum(dc), column_sum(d4.astype(F32)), column_sum(dbranch.astype(F32))]
    add_to(g_vec_ref, step, jnp.concatenate(rows + [jnp.zeros((4, WIDTH), F32)], axis=0))


def feed_backward(grad, keep, weights, vectors, u3, last):
    operands = (grad, u3, last, vectors, weights["up"], weights["up_t"], weights["down_t"], weights["out_t"])
    specs = [whole(x.shape) for x in operands]
    specs[1] = rows_of(WIDTH)
    specs[2] = rows_of(WIDTH)
    outs = [(PIX, WIDTH), (2, EARLY_ROWS, 128), (WIDTH, WIDTH), (8, WIDTH)]
    return pl.pallas_call(
        feed_backward_kernel,
        grid=(CHUNKS,),
        in_specs=[in_smem()] + specs,
        out_specs=[rows_of(WIDTH)] + [whole(s) for s in outs[1:]],
        out_shape=[jax.ShapeDtypeStruct(s, F32) for s in outs],
        scratch_shapes=[pltpu.VMEM((CLIP, OWN, WIDTH), F32)],
        compiler_params=pltpu.CompilerParams(vmem_limit_bytes=VMEM_LIMIT),
        name="feed_backward",
    )(keep, *operands)


def attend_back_chunk(qkv, d_mixture, bias):
    out = []
    for group in range(CHUNK // GROUP):
        rows = slice(group * GROUP, (group + 1) * GROUP)
        grads = [[], [], []]
        for pair in range(HEADS // 2):
            lanes = pair * 2 * SLOT
            queries = qkv[rows, lanes : lanes + GROUP]
            keys = lane_halves(qkv[rows, SLOTS + lanes : SLOTS + lanes + GROUP])
            values = lane_halves(qkv[rows, 2 * SLOTS + lanes : 2 * SLOTS + lanes + GROUP])
            d_out = d_mixture[rows, lanes : lanes + GROUP]
            scores = dot_nt(keys, queries) * SCALE + bias
            d_probs = dot_nt(values, d_out)
            low_probs = []
            d_scores = []
            for head in range(2):
                part = scores[head * GROUP : (head + 1) * GROUP]
                d_part = d_probs[head * GROUP : (head + 1) * GROUP]
                raised = jnp.exp(part - jnp.max(part, axis=0, keepdims=True))
                probs = raised * (1.0 / jnp.sum(raised, axis=0, keepdims=True))
                low_probs.append(to_low(probs))
                d_scores.append(to_low(probs * (d_part - jnp.sum(probs * d_part, axis=0, keepdims=True))))
            low_probs = jnp.concatenate(low_probs, axis=0)
            d_scores = jnp.concatenate(d_scores, axis=0)
            d_values = dot(low_probs, d_out)
            d_keys = dot(d_scores, queries) * SCALE
            d_queries = dot_tn(d_scores, keys) * SCALE
            lane = lax.broadcasted_iota(jnp.int32, (GROUP, GROUP), 1)
            grads[0].append(to_low(d_queries))
            grads[1].append(to_low(jnp.where(lane < SLOT, d_keys[:GROUP], d_keys[GROUP:])))
            grads[2].append(to_low(jnp.where(lane < SLOT, d_values[:GROUP], d_values[GROUP:])))
        out.append(jnp.concatenate(grads[0] + grads[1] + grads[2], axis=1))
    return jnp.concatenate(out, axis=0)


def attention_backward_step(step, count, grad, stream, qkv, mixture, codes, gain, offset, t_o, t_qkv, sel_t, g_refs):
    bias = key_bias(count, False)
    d_out = to_low(grad)
    padded = dot_tn(mixture, d_out)
    w_o_grad = jnp.concatenate([padded[head * SLOT : head * SLOT + HEAD_DIM] for head in range(HEADS)], axis=0)
    add_to(g_refs[3], step, w_o_grad)
    d_mixture = to_low(dot(d_out, t_o))
    d_qkv = attend_back_chunk(qkv, d_mixture, bias)
    normal, scale = normal_parts(stream)
    a = to_low(normal * gain + offset + codes)
    for j in range(3):
        tight = to_low(dot(d_qkv[:, j * SLOTS : (j + 1) * SLOTS], sel_t))
        add_to(g_refs[j], step, dot_tn(a, tight))
    d_a = dot(d_qkv, t_qkv)
    rows = [column_sum(d_a * normal), column_sum(d_a), column_sum(d_out.astype(F32))]
    return grad + normal_back(d_a, normal, scale, gain), rows


def second_backward_kernel(
    count_ref, grad_ref, u2_ref, qkv_ref, o_ref, codes_ref, vec_ref, t_o_ref, t_qkv_ref, sel_t_ref,
    du2_ref, gq_ref, gk_ref, gv_ref, go_ref, g_vec_ref,
):
    step = pl.program_id(0)
    du2, rows = attention_backward_step(
        step, count_ref[0], grad_ref[...], u2_ref[...], qkv_ref[...], o_ref[...], codes_ref[...],
        vec_ref[6:7, :], vec_ref[7:8, :], t_o_ref[...], t_qkv_ref[...], sel_t_ref[...], (gq_ref, gk_ref, gv_ref, go_ref),
    )
    du2_ref[...] = du2
    add_to(g_vec_ref, step, jnp.concatenate(rows + [jnp.zeros((5, WIDTH), F32)], axis=0))


def second_backward(grad, count, weights, vectors, u2, qkv, mixture):
    operands = (grad, u2, qkv, mixture, frame_codes(), vectors, weights["o_t"][1], weights["qkv_t"][1], slot_selector().T)
    specs = [rows_of(WIDTH), rows_of(WIDTH), rows_of(3 * SLOTS), rows_of(SLOTS)] + [whole(x.shape) for x in operands[4:]]
    outs = [(PIX, WIDTH)] + [(WIDTH, WIDTH)] * 4 + [(8, WIDTH)]
    return pl.pallas_call(
        second_backward_kernel,
        grid=(CHUNKS,),
        in_specs=[in_smem()] + specs,
        out_specs=[rows_of(WIDTH)] + [whole(s) for s in outs[1:]],
        out_shape=[jax.ShapeDtypeStruct(s, F32) for s in outs],
        compiler_params=pltpu.CompilerParams(vmem_limit_bytes=VMEM_LIMIT),
        name="second_backward",
    )(count, *operands)


def first_backward_kernel(
    count_ref, loss_ref, grad_ref, u_ref, qkv_ref, o_ref, arrived_ref, codes_ref, vec_ref, t_o_ref, t_qkv_ref, sel_t_ref, t_in_ref,
    g5_ref, g6_ref, g7_ref, g8_ref, g9_ref, feed_vec_ref, second_vec_ref,
    packed_ref,
    wide, g0, g1, g2, g3, g4, sums,
):
    step = pl.program_id(0)

    @pl.when(step == 0)
    def _():
        unpack_positions(arrived_ref, wide)

    du, rows = attention_backward_step(
        step, count_ref[0], grad_ref[...], u_ref[...], qkv_ref[...], o_ref[...], codes_ref[...],
        vec_ref[3:4, :], vec_ref[4:5, :], t_o_ref[...], t_qkv_ref[...], sel_t_ref[...], (g1, g2, g3, g4),
    )
    du = to_low(du)
    normed = chunk_tokens(wide, step)
    inputs = to_low(normed * vec_ref[0:1, :] + vec_ref[1:2, :])
    add_to(g0, step, dot_tn(inputs, du))
    d_inputs = dot(du, t_in_ref[...])
    top = [column_sum(d_inputs * normed), column_sum(d_inputs), column_sum(du.astype(F32))]
    add_to(sums, step, jnp.concatenate(top + rows + [jnp.zeros((2, WIDTH), F32)], axis=0))

    @pl.when(step == CHUNKS - 1)
    def _():
        squares = (g0, g1, g2, g3, g4, g5_ref, g6_ref, g7_ref, g8_ref, g9_ref)
        vector_rows = jnp.concatenate(
            [sums[0:6, :], second_vec_ref[0:3, :], feed_vec_ref[0:4, :], jnp.full((3, WIDTH), loss_ref[0])], axis=0
        )
        pieces = [vector_rows[:, 64 * j : 64 * (j + 1)] for j in range(5)]
        side = jnp.concatenate(pieces + [jnp.zeros((WIDTH - 80, 64), F32)], axis=0)
        for half in range(2):
            own = squares[5 * half : 5 * half + 5]
            for index in range(5):
                packed_ref[half, tile_rows(2 * index)] = own[index][:, 0:128]
                packed_ref[half, tile_rows(2 * index + 1)] = own[index][:, 128:256]
            for pair in range(2):
                packed_ref[half, tile_rows(10 + pair)] = jnp.concatenate(
                    [own[2 * pair][:, 256:320], own[2 * pair + 1][:, 256:320]], axis=1
                )
            packed_ref[half, 13 * WIDTH :] = jnp.zeros((LATE_ROWS - 13 * WIDTH, 128), F32)
            packed_ref[half, tile_rows(12)] = jnp.concatenate([own[4][:, 256:320], side], axis=1)


def first_backward(grad, count, loss_part, arrived, weights, vectors, u, qkv, mixture, later):
    operands = (
        grad, u, qkv, mixture, arrived, frame_codes(), vectors, weights["o_t"][0], weights["qkv_t"][0], slot_selector().T, weights["in_t"],
    ) + tuple(later)
    specs = [rows_of(WIDTH), rows_of(WIDTH), rows_of(3 * SLOTS), rows_of(SLOTS)] + [whole(x.shape) for x in operands[4:]]
    return pl.pallas_call(
        first_backward_kernel,
        grid=(CHUNKS,),
        in_specs=[in_smem(), in_smem()] + specs,
        out_specs=whole((2, LATE_ROWS, 128)),
        out_shape=jax.ShapeDtypeStruct((2, LATE_ROWS, 128), F32),
        scratch_shapes=[pltpu.VMEM((CLIP, OWN, WIDTH), F32)] + [pltpu.VMEM((WIDTH, WIDTH), F32)] * 5 + [pltpu.VMEM((8, WIDTH), F32)],
        compiler_params=pltpu.CompilerParams(vmem_limit_bytes=VMEM_LIMIT),
        name="first_backward",
    )(count, loss_part, *operands)


MUON_RATE = 0.2
ADAM_RATE = 0.4
DECAY = 0.01
AVERAGE = 0.75
STEP = 10
SHRINK = 1.0 - MUON_RATE * DECAY
SQUARE_RATE = MUON_RATE * 0.2 * math.sqrt(WIDTH)
UP_RATE = MUON_RATE * 0.2 * math.sqrt(2 * FF_INNER)
DOWN_RATE = MUON_RATE * 0.2 * math.sqrt(FF_INNER)
UP_TILES = 10
DOWN_TILES = 5
WIDE_TILES = 2 * UP_TILES
EARLY_ROWS = 4864
LATE_ROWS = 4224


def tile_rows(index):
    return slice(index * WIDTH, (index + 1) * WIDTH)


def halves(values):
    high = values.astype(BF16)
    return (high, (values - high.astype(F32)).astype(BF16))


def triple(left, right, transposed=False):
    stacked = jnp.concatenate([left[0], left[0], left[1]], axis=1)
    if transposed:
        return dot_nt(stacked, jnp.concatenate([right[0], right[1], right[0]], axis=1))
    return dot(stacked, jnp.concatenate([right[0], right[1], right[0]], axis=0))


def scaled_to_unit(matrix):
    return matrix * (1.0 / (jnp.sqrt(jnp.sum(matrix * matrix, keepdims=True)) + 1e-07))


def wide_moments_kernel(sum_ref, up_ref, down_ref, up_new_ref, down_new_ref, ahead_ref):
    for tile in range(UP_TILES):
        lanes = slice(128 * tile, 128 * (tile + 1))
        gradient = sum_ref[tile_rows(tile)]
        moment = 0.95 * up_ref[:, lanes] + gradient
        up_new_ref[:, lanes] = moment
        ahead_ref[tile] = gradient + 0.95 * moment
    for tile in range(DOWN_TILES):
        rows = slice(128 * tile, 128 * (tile + 1))
        gradient = sum_ref[tile_rows(UP_TILES + tile)]
        moment = 0.95 * down_ref[rows, :] + gradient.T
        down_new_ref[rows, :] = moment
        ahead_ref[UP_TILES + tile] = gradient + 0.95 * moment.T


def wide_moments(summed, up_moment, down_moment):
    return pl.pallas_call(
        wide_moments_kernel,
        in_specs=[in_vmem()] * 3,
        out_specs=[in_vmem()] * 3,
        out_shape=[
            jax.ShapeDtypeStruct(up_moment.shape, F32),
            jax.ShapeDtypeStruct(down_moment.shape, F32),
            jax.ShapeDtypeStruct((UP_TILES + DOWN_TILES, WIDTH, 128), F32),
        ],
        compiler_params=pltpu.CompilerParams(vmem_limit_bytes=VMEM_LIMIT),
        name="wide_moments",
    )(summed, up_moment, down_moment)


def wide_direction_kernel(core_ref, own_ref, got_ref, o_ref, matrix):
    def put(tile, value):
        matrix[:, 128 * tile : 128 * (tile + 1)] = value

    @pl.when(core_ref[0] == 0)
    def _():
        for tile in range(UP_TILES):
            put(tile, own_ref[tile])
            put(UP_TILES + tile, got_ref[tile])

    @pl.when(core_ref[0] != 0)
    def _():
        for tile in range(DOWN_TILES):
            put(tile, got_ref[UP_TILES - DOWN_TILES + tile])
            put(DOWN_TILES + tile, own_ref[UP_TILES + tile])
        matrix[:, 128 * UP_TILES :] = jnp.zeros((WIDTH, 128 * UP_TILES), F32)

    parts = halves(scaled_to_unit(matrix[...]))
    gram = triple(parts, parts, True)
    row = lax.broadcasted_iota(jnp.int32, (WIDTH, WIDTH), 0)
    column = lax.broadcasted_iota(jnp.int32, (WIDTH, WIDTH), 1)
    total = None
    for step in range(5):
        gram_parts = halves(gram)
        polynomial = -4.775 * gram + 2.0315 * triple(gram_parts, gram_parts)
        poly_parts = halves(polynomial)
        if total is None:
            total = polynomial + jnp.where(row == column, 3.4445, 0.0)
        else:
            total = 3.4445 * total + triple(poly_parts, halves(total))
        if step < 4:
            once = 3.4445 * gram + triple(poly_parts, gram_parts)
            gram = 3.4445 * once + triple(halves(once), poly_parts)
    direction = to_low(triple(halves(total), parts))
    for tile in range(WIDE_TILES):
        o_ref[tile] = direction[:, 128 * tile : 128 * (tile + 1)]


def wide_direction(core, own, got):
    return pl.pallas_call(
        wide_direction_kernel,
        in_specs=[in_smem(), in_vmem(), in_vmem()],
        out_specs=in_vmem(),
        out_shape=jax.ShapeDtypeStruct((WIDE_TILES, WIDTH, 128), BF16),
        scratch_shapes=[pltpu.VMEM((WIDTH, 128 * WIDE_TILES), F32)],
        compiler_params=pltpu.CompilerParams(vmem_limit_bytes=VMEM_LIMIT),
        name="wide_direction",
    )(core, own, got)


def wide_update_kernel(
    core_ref, own_ref, got_ref, up_ref, down_ref, up_ema_ref, down_ema_ref,
    up_new_ref, up_ema_new_ref, down_new_ref, down_ema_new_ref,
):
    def update(up_dir, down_dir):
        for tile in range(WIDE_TILES):
            lanes = slice(128 * tile, 128 * (tile + 1))
            up_new_ref[:, lanes] = up_ref[:, lanes] * SHRINK - UP_RATE * up_dir[tile].astype(F32)
        for tile in range(2 * DOWN_TILES):
            rows = slice(128 * tile, 128 * (tile + 1))
            down_new_ref[rows, :] = down_ref[rows, :] * SHRINK - DOWN_RATE * down_dir[tile].astype(F32).T

    def average(half):
        lanes = slice(128 * UP_TILES * half, 128 * UP_TILES * (half + 1))
        up_ema_new_ref[...] = AVERAGE * up_ema_ref[...] + (1.0 - AVERAGE) * up_new_ref[:, lanes]
        rows = slice(128 * DOWN_TILES * half, 128 * DOWN_TILES * (half + 1))
        down_ema_new_ref[...] = AVERAGE * down_ema_ref[...] + (1.0 - AVERAGE) * down_new_ref[rows, :]

    @pl.when(core_ref[0] == 0)
    def _():
        update(own_ref, got_ref)
        average(0)

    @pl.when(core_ref[0] != 0)
    def _():
        update(got_ref, own_ref)
        average(1)


def wide_update(core, own, got, up, down, up_ema, down_ema):
    return pl.pallas_call(
        wide_update_kernel,
        in_specs=[in_smem()] + [in_vmem()] * 6,
        out_specs=[in_vmem()] * 4,
        out_shape=[jax.ShapeDtypeStruct(x.shape, F32) for x in (up, up_ema, down, down_ema)],
        compiler_params=pltpu.CompilerParams(vmem_limit_bytes=VMEM_LIMIT),
        name="wide_update",
    )(core, own, got, up, down, up_ema, down_ema)


def square_directions_kernel(
    sum_ref, moment_ref, m1_ref, m2_ref, vec_ref, vec_ema_ref,
    direction_ref, moment_new_ref, m1_new_ref, m2_new_ref, vec_new_ref, vec_ema_new_ref, loss_ref,
    matrix,
):
    side = sum_ref[tile_rows(12)][:, 64:128]
    rows = jnp.concatenate([side[16 * j : 16 * (j + 1)] for j in range(5)], axis=1)
    loss_ref[...] = rows[13:14, 0:128]
    gradient = rows[0:13]
    first = 0.9 * m1_ref[...] + 0.1 * gradient
    second = 0.999 * m2_ref[...] + 0.001 * (gradient * gradient)
    m1_new_ref[...] = first
    m2_new_ref[...] = second
    adjusted = first * (1.0 / (1.0 - 0.9**STEP)) / (jnp.sqrt(second * (1.0 / (1.0 - 0.999**STEP))) + 1e-08)
    fresh = vec_ref[...] - ADAM_RATE * (adjusted + DECAY * vec_ref[...])
    vec_new_ref[...] = fresh
    vec_ema_new_ref[...] = AVERAGE * vec_ema_ref[...] + (1.0 - AVERAGE) * fresh
    for index in range(5):
        lanes = slice(64 * (index % 2), 64 * (index % 2) + 64)
        gradient = jnp.concatenate(
            [sum_ref[tile_rows(2 * index)], sum_ref[tile_rows(2 * index + 1)], sum_ref[tile_rows(10 + index // 2)][:, lanes]],
            axis=1,
        )
        moment = 0.95 * moment_ref[index] + gradient
        moment_new_ref[index] = moment
        matrix[index] = scaled_to_unit(gradient + 0.95 * moment)

    def step(_, carry):
        for index in range(5):
            current = matrix[index]
            parts = halves(current)
            gram = triple(parts, parts, True)
            gram_parts = halves(gram)
            polynomial = -4.775 * gram + 2.0315 * triple(gram_parts, gram_parts)
            matrix[index] = 3.4445 * current + triple(halves(polynomial), parts)
        return carry

    lax.fori_loop(0, 5, step, 0)
    direction_ref[...] = to_low(matrix[...])


def square_directions(summed, moment, m1, m2, vectors, vec_ema):
    shapes = [(moment.shape, BF16), (moment.shape, F32)] + [(vectors.shape, F32)] * 4 + [((1, 128), F32)]
    return pl.pallas_call(
        square_directions_kernel,
        in_specs=[in_vmem()] * 6,
        out_specs=[in_vmem()] * 7,
        out_shape=[jax.ShapeDtypeStruct(s, d) for s, d in shapes],
        scratch_shapes=[pltpu.VMEM(moment.shape, F32)],
        compiler_params=pltpu.CompilerParams(vmem_limit_bytes=VMEM_LIMIT),
        name="square_directions",
    )(summed, moment, m1, m2, vectors, vec_ema)


def square_update_kernel(core_ref, own_ref, got_ref, weight_ref, ema_ref, new_ref, ema_new_ref):
    def update(half, direction):
        for index in range(5):
            new_ref[5 * half + index] = weight_ref[5 * half + index] * SHRINK - SQUARE_RATE * direction[index].astype(F32)

    def average(half):
        for index in range(5):
            ema_new_ref[index] = AVERAGE * ema_ref[index] + (1.0 - AVERAGE) * new_ref[5 * half + index]

    for core in range(2):

        @pl.when(core_ref[0] == core)
        def _(core=core):
            update(core, own_ref)
            update(1 - core, got_ref)
            average(core)


def square_update(core, own, got, weights, ema):
    return pl.pallas_call(
        square_update_kernel,
        in_specs=[in_smem()] + [in_vmem()] * 4,
        out_specs=[in_vmem()] * 2,
        out_shape=[jax.ShapeDtypeStruct(x.shape, F32) for x in (weights, ema)],
        compiler_params=pltpu.CompilerParams(vmem_limit_bytes=VMEM_LIMIT),
        name="square_update",
    )(core, own, got, weights, ema)


TAPS = 9
CHAN = 4


def group_ones():
    group = np.arange(WIDTH) // (WIDTH // GN_GROUPS)
    return jnp.asarray((group[:, None] == group[None, :]).astype(np.float32), BF16)


def group_mean(column_sums, ones):
    rest = jnp.broadcast_to(column_sums, (8, WIDTH))
    total = jnp.zeros((8, WIDTH), F32)
    for _ in range(3):
        part = to_low(rest)
        total = total + dot(part, ones)
        rest = rest - part.astype(F32)
    return total[0:1] * (1.0 / (PIX * (WIDTH // GN_GROUPS)))


def chunk_rows(index):
    return pl.ds(pl.multiple_of(index * CHUNK, CHUNK), CHUNK)


def over_chunks(body, *start):
    return lax.fori_loop(0, CHUNKS, lambda i, carry: body(i, *carry), start)


def zero_row():
    return jnp.zeros((1, WIDTH), F32)


def group_stats(ref, ones, column_sums):
    centre = group_mean(column_sums, ones)

    def squares(i, total):
        shifted = ref[chunk_rows(i), :] - centre
        return (total + column_sum(shifted * shifted),)

    (total,) = over_chunks(squares, zero_row())
    return centre, lax.rsqrt(group_mean(total, ones) + 1e-05)


def sigmoid(values):
    return 1.0 / (1.0 + jnp.exp(-values))


def shifted_lanes(values, down, right):
    lane = lax.broadcasted_iota(jnp.int32, values.shape, 1)
    line = lane // LATENT + down
    place = lane % LATENT + right
    inside = (line >= 0) & (line < LATENT) & (place >= 0) & (place < LATENT)
    offset = (down * LATENT + right) % PIX
    moved = pltpu.roll(values, (PIX - offset) % PIX, 1) if offset else values
    return jnp.where(inside, moved, 0.0)


def put_columns(cols_ref, act_ref):
    zeros = jnp.zeros((LATENT, 3 * WIDTH), BF16)
    cols_ref[0:LATENT, :] = zeros
    cols_ref[LATENT + PIX :, :] = zeros
    act_ref[0:8, :] = jnp.zeros((8, WIDTH), F32)
    act_ref[8 + PIX :, :] = jnp.zeros((8, WIDTH), F32)

    for i in range(CHUNKS):
        place = (lax.broadcasted_iota(jnp.int32, (CHUNK, WIDTH), 0)) % LATENT
        middle = act_ref[8 + i * CHUNK : 8 + (i + 1) * CHUNK, :]
        left = act_ref[7 + i * CHUNK : 7 + (i + 1) * CHUNK, :]
        right = act_ref[9 + i * CHUNK : 9 + (i + 1) * CHUNK, :]
        left = jnp.where(place == 0, 0.0, left)
        right = jnp.where(place == LATENT - 1, 0.0, right)
        cols_ref[LATENT + i * CHUNK : LATENT + (i + 1) * CHUNK, :] = jnp.concatenate(
            [to_low(left), to_low(middle), to_low(right)], axis=1
        )


def resnet_kernel(
    noisy_ref, vec_ref, temb_ref, ones_ref, w_in_ref, w_res_ref, w_s0_ref,
    resnet_ref, tokens_ref,
    first, inner, act, cols,
):
    ones = ones_ref[...]

    def vec(i):
        return vec_ref[i : i + 1, :]

    noisy = noisy_ref[...]
    taps = [shifted_lanes(noisy, tap // 3 - 1, tap % 3 - 1) for tap in range(TAPS)]
    columns = to_low(jnp.concatenate(taps, axis=0))
    w_in = w_in_ref[...]
    total = zero_row()
    for i in range(CHUNKS):
        part = dot_tn(columns[:, i * CHUNK : (i + 1) * CHUNK], w_in) + vec(0)
        first[i * CHUNK : (i + 1) * CHUNK, :] = part
        total = total + column_sum(part)

    def activate(source, total, gain, offset):
        centre, scale = group_stats(source, ones, total)

        def one(i):
            normal = (source[chunk_rows(i), :] - centre) * scale * gain + offset
            act[pl.ds(pl.multiple_of(8 + i * CHUNK, 8), CHUNK), :] = normal * sigmoid(normal)
            return ()

        over_chunks(lambda i: one(i))
        put_columns(cols, act)

    def convolve_chunk(i, which):
        out = None
        for line in range(3):
            part = cols[pl.ds(pl.multiple_of(i * CHUNK + LATENT * line, LATENT), CHUNK), :]
            term = dot(part, w_res_ref[which, line])
            out = term if out is None else out + term
        return out

    activate(first, total, vec(1), vec(2))
    shift = vec(3) + temb_ref[...]

    def first_step(i, total):
        part = convolve_chunk(i, 0) + shift
        inner[chunk_rows(i), :] = part
        return (total + column_sum(part),)

    (total,) = over_chunks(first_step, zero_row())
    activate(inner, total, vec(4), vec(5))

    def second_step(i, total):
        part = first[chunk_rows(i), :] + (convolve_chunk(i, 1) + vec(6))
        resnet_ref[chunk_rows(i), :] = part
        return (total + column_sum(part),)

    (total,) = over_chunks(second_step, zero_row())
    centre, scale = group_stats(resnet_ref, ones, total)

    def token_step(i):
        normal = to_low((resnet_ref[chunk_rows(i), :] - centre) * scale * vec(7) + vec(8))
        tokens_ref[chunk_rows(i), :] = dot(normal, w_s0_ref[...]) + vec(9)
        return ()

    over_chunks(lambda i: token_step(i))


def resnet_block(noisy, vectors, temb, w_in, w_res, w_s0):
    return pl.pallas_call(
        resnet_kernel,
        in_specs=[in_vmem()] * 7,
        out_specs=[in_vmem()] * 2,
        out_shape=[jax.ShapeDtypeStruct((PIX, WIDTH), F32)] * 2,
        scratch_shapes=[
            pltpu.VMEM((PIX, WIDTH), F32),
            pltpu.VMEM((PIX, WIDTH), F32),
            pltpu.VMEM((PIX + 16, WIDTH), F32),
            pltpu.VMEM((PIX + 2 * LATENT, 3 * WIDTH), BF16),
        ],
        compiler_params=pltpu.CompilerParams(vmem_limit_bytes=VMEM_LIMIT),
        name="resnet_block",
    )(noisy, vectors, temb, group_ones(), w_in, w_res, w_s0)


def prepare_spatial_kernel(sq_ref, sel_ref, w_qkv, w_o, w_q2, w_o2):
    sel = sel_ref[...]
    for j in range(3):
        w_qkv[:, j * SLOTS : (j + 1) * SLOTS] = to_low(dot(sq_ref[1 + j], sel))
    w_q2[...] = to_low(dot(sq_ref[5], sel))
    w_o[...] = to_low(dot_tn(sel, sq_ref[4]))
    w_o2[...] = to_low(dot_tn(sel, sq_ref[6]))


def prepare_spatial(squares):
    shapes = [(WIDTH, 3 * SLOTS), (SLOTS, WIDTH), (WIDTH, SLOTS), (SLOTS, WIDTH)]
    return pl.pallas_call(
        prepare_spatial_kernel,
        in_specs=[in_vmem()] * 2,
        out_specs=[in_vmem()] * 4,
        out_shape=[jax.ShapeDtypeStruct(s, BF16) for s in shapes],
        compiler_params=pltpu.CompilerParams(vmem_limit_bytes=VMEM_LIMIT),
        name="spatial_weights",
    )(squares, slot_selector())


LOG2E = 1.4426950408889634
TEXT_ROWS = 128


def transformer_kernel(
    tokens_ref, resnet_ref, text_ref, vec_ref, ones_ref, sel_ref, w_qkv_ref, w_o_ref, w_q2_ref, w_kv2_ref, w_o2_ref,
    w_up_ref, w_down_ref, w_s7_ref,
    hidden_ref, packed_ref,
    queries, keys, values, text_kv,
):
    def vec(i):
        return vec_ref[i : i + 1, :]

    lane = lax.broadcasted_iota(jnp.int32, (CHUNK, SLOTS), 1)
    counter = jnp.where(lane % SLOT == HEAD_DIM, 1.0, 0.0)

    def project(i):
        a = to_low(normal_parts(tokens_ref[chunk_rows(i), :])[0] * vec(10) + vec(11))
        qkv = dot(a, w_qkv_ref[...])
        queries[chunk_rows(i), :] = to_low(qkv[:, :SLOTS])
        keys[chunk_rows(i), :] = to_low(qkv[:, SLOTS : 2 * SLOTS])
        values[chunk_rows(i), :] = to_low(qkv[:, 2 * SLOTS :] + counter)
        return ()

    over_chunks(lambda i: project(i))
    kv = to_low(dot(text_ref[...], w_kv2_ref[...]))
    text_kv[...] = jnp.zeros_like(text_kv)
    wide_kv = jnp.concatenate(
        [dot(kv[:, :WIDTH], sel_ref[...]), dot(kv[:, WIDTH:], sel_ref[...])], axis=1
    )
    text_kv[0 : wide_kv.shape[0], :] = wide_kv
    text_lane = lax.broadcasted_iota(jnp.int32, (CHUNK, TEXT_ROWS), 1)
    text_bias = jnp.where(text_lane < TEXT_LEN, 0.0, -1e30)

    def chunk_step(i, total):
        tokens = tokens_ref[chunk_rows(i), :]
        pairs = []
        for pair in range(HEADS // 2):
            lanes = slice(pair * GROUP, (pair + 1) * GROUP)
            query = queries[chunk_rows(i), lanes]
            key = keys[:, lanes]
            value = values[:, lanes]
            side = lax.broadcasted_iota(jnp.int32, (CHUNK, GROUP), 1) < SLOT
            both = None
            for head in range(2):
                zero = jnp.zeros_like(query)
                own_query = jnp.where(side, query, zero) if head == 0 else jnp.where(side, zero, query)
                scores = dot_nt(own_query, key) * (SCALE * LOG2E)
                raised = jnp.exp2(scores - jnp.max(scores, axis=1, keepdims=True))
                mixed = dot(to_low(raised), value)
                mixed = mixed * (1.0 / mixed[:, head * SLOT + HEAD_DIM : head * SLOT + HEAD_DIM + 1])
                both = mixed if head == 0 else jnp.where(side, both, mixed)
            pairs.append(to_low(both))
        tokens = tokens + (dot(jnp.concatenate(pairs, axis=1), w_o_ref[...]) + vec(12))
        c = to_low(normal_parts(tokens)[0] * vec(13) + vec(14))
        query2 = to_low(dot(c, w_q2_ref[...]))
        pairs = []
        for pair in range(HEADS // 2):
            lanes = slice(pair * GROUP, (pair + 1) * GROUP)
            text_keys = lane_halves(to_low(text_kv[:, lanes]))
            text_values = lane_halves(to_low(text_kv[:, SLOTS + pair * GROUP : SLOTS + (pair + 1) * GROUP]))
            scores = dot_nt(query2[:, lanes], text_keys) * SCALE
            probs = []
            for part in (scores[:, :TEXT_ROWS], scores[:, TEXT_ROWS:]):
                part = part + text_bias
                raised = jnp.exp(part - jnp.max(part, axis=1, keepdims=True))
                probs.append(to_low(raised * (1.0 / jnp.sum(raised, axis=1, keepdims=True))))
            pairs.append(to_low(dot(jnp.concatenate(probs, axis=1), text_values)))
        tokens = tokens + (dot(jnp.concatenate(pairs, axis=1), w_o2_ref[...]) + vec(15))
        f = to_low(normal_parts(tokens)[0] * vec(16) + vec(17))
        gate_up = dot(f, w_up_ref[...])
        inner = to_low(gate_up[:, :FF_INNER] * gelu_parts(gate_up[:, FF_INNER:])[0])
        tokens = tokens + (dot(inner, w_down_ref[...]) + vec(18))
        hidden = resnet_ref[chunk_rows(i), :] + (dot(to_low(tokens), w_s7_ref[...]) + vec(19))
        hidden_ref[chunk_rows(i), :] = hidden
        return (total + column_sum(hidden),)

    (total,) = over_chunks(chunk_step, zero_row())
    centre, scale = group_stats(hidden_ref, ones_ref[...], total)
    pack_rows(packed_ref, lambda rows: (hidden_ref[rows, :] - centre) * scale)


def pack_rows(packed_ref, rows_at):
    for member in range(CLIP):
        block = to_low(rows_at(slice(member * OWN, (member + 1) * OWN)))
        packed_ref[member, 0:64, :] = block[:, 0:128]
        packed_ref[member, 64:128, :] = block[:, 128:256]
        packed_ref[member, 128:160, :] = jnp.concatenate([block[0:32, 256:320], block[32:64, 256:320]], axis=1)


def transformer_block(tokens, resnet, text, vectors, prepared, cross_kv, up, down, w_s7):
    w_qkv, w_o, w_q2, w_o2 = prepared
    operands = (
        tokens, resnet, text, vectors, group_ones(), slot_selector(), w_qkv, w_o, w_q2, cross_kv, w_o2, up, down, w_s7,
    )
    return pl.pallas_call(
        transformer_kernel,
        in_specs=[in_vmem()] * len(operands),
        out_specs=[in_vmem()] * 2,
        out_shape=[
            jax.ShapeDtypeStruct((PIX, WIDTH), F32),
            jax.ShapeDtypeStruct((CLIP, 160, 128), BF16),
        ],
        scratch_shapes=[pltpu.VMEM((PIX, SLOTS), BF16)] * 3 + [pltpu.VMEM((TEXT_ROWS, 2 * SLOTS), F32)],
        compiler_params=pltpu.CompilerParams(vmem_limit_bytes=VMEM_LIMIT),
        name="transformer_block",
    )(*operands)


def head_kernel(
    valid_ref, total_ref, hidden_ref, branch_ref, target_ref, vec_ref, ones_ref, w_ref,
    packed_ref, loss_ref,
    mixed, act, slope,
):
    ones = ones_ref[...]
    gain = vec_ref[20:21, :]
    offset = vec_ref[21:22, :]
    column_total = zero_row()
    for member in range(CLIP):
        rows = slice(member * OWN, (member + 1) * OWN)
        last = branch_ref[member, 128:160, :]
        branch = jnp.concatenate(
            [
                branch_ref[member, 0:64, :].astype(F32),
                branch_ref[member, 64:128, :].astype(F32),
                jnp.concatenate([last[:, 0:64], last[:, 64:128]], axis=0).astype(F32),
            ],
            axis=1,
        )
        part = hidden_ref[rows, :] + branch
        mixed[rows, :] = part
        column_total = column_total + column_sum(part)
    centre, scale = group_stats(mixed, ones, column_total)

    def activate(i):
        normal = (mixed[chunk_rows(i), :] - centre) * scale
        mixed[chunk_rows(i), :] = normal
        value = normal * gain + offset
        share = sigmoid(value)
        act[chunk_rows(i), :] = to_low(value * share)
        slope[chunk_rows(i), :] = share * (1.0 + value * (1.0 - share)) * gain
        return ()

    over_chunks(lambda i: activate(i))
    weight = w_ref[...]
    by_tap = dot_nt(weight, act[...])
    predicted = jnp.zeros((8, PIX), F32)
    for tap in range(TAPS):
        predicted = predicted + shifted_lanes(by_tap[8 * tap : 8 * tap + 8], tap // 3 - 1, tap % 3 - 1)
    residual = (predicted - target_ref[...]) * valid_ref[0]
    loss_ref[...] = jnp.sum(residual * residual, keepdims=True)
    grad = to_low(2.0 * residual / total_ref[0]).astype(F32)
    columns = to_low(jnp.concatenate([shifted_lanes(grad, 1 - tap // 3, 1 - tap % 3) for tap in range(TAPS)], axis=0))
    total = zero_row()
    total_normal = zero_row()
    for i in range(CHUNKS):
        rows = slice(i * CHUNK, (i + 1) * CHUNK)
        part = dot_tn(columns[:, rows], weight) * slope[rows, :]
        slope[rows, :] = part
        total = total + column_sum(part)
        total_normal = total_normal + column_sum(part * mixed[rows, :])
    mean = group_mean(total, ones)
    mean_normal = group_mean(total_normal, ones)
    pack_rows(packed_ref, lambda rows: scale * (slope[rows, :] - mean - mixed[rows, :] * mean_normal))


def head_block(valid, total, hidden, branch, target, vectors, weight):
    return pl.pallas_call(
        head_kernel,
        in_specs=[in_smem(), in_smem()] + [in_vmem()] * 6,
        out_specs=[in_vmem()] * 2,
        out_shape=[jax.ShapeDtypeStruct((CLIP, 160, 128), BF16), jax.ShapeDtypeStruct((1, 1), F32)],
        scratch_shapes=[
            pltpu.VMEM((PIX, WIDTH), F32),
            pltpu.VMEM((PIX, WIDTH), BF16),
            pltpu.VMEM((PIX, WIDTH), F32),
        ],
        compiler_params=pltpu.CompilerParams(vmem_limit_bytes=VMEM_LIMIT),
        name="head_block",
    )(valid, total, hidden, branch, target, vectors, group_ones(), weight)


def product(left, right):
    return jnp.einsum("...i,ij->...j", left, right, preferred_element_type=jnp.float32)


def time_embed(step_values, time_w1, time_w2, temb_w, temb_bias):
    half_width = WIDTH // 2
    frequency = jnp.exp(-math.log(10000.0) * jnp.arange(half_width, dtype=jnp.float32) / half_width)
    angles = step_values[..., None] * frequency
    encoding = jnp.concatenate([jnp.cos(angles), jnp.sin(angles)], axis=-1)
    hidden = product(to_low(encoding), time_w1)
    hidden = product(to_low(jax.nn.silu(hidden)), time_w2)
    return product(to_low(jax.nn.silu(hidden)), temb_w) + temb_bias


def swap_cores(values):
    return lax.ppermute(values, "dp", [(0, 1), (1, 0)])


def frames_bit(bit):
    return (lax.axis_index("frames") // bit) % 2


def swap_frames(values, bit):
    size = lax.axis_size("frames")
    return lax.ppermute(values, "frames", [(i, i ^ bit) for i in range(size)])


def sum_over_frames(values, order):
    for bit in order:
        rows = values.shape[0] // 2
        mine = frames_bit(bit)
        own = lax.dynamic_slice_in_dim(values, mine * rows, rows, 0)
        other = lax.dynamic_slice_in_dim(values, (1 - mine) * rows, rows, 0)
        values = own + swap_frames(other, bit)
    for bit in reversed(order):
        got = swap_frames(values, bit)
        values = jnp.where(
            frames_bit(bit) == 0,
            jnp.concatenate([values, got], 0),
            jnp.concatenate([got, values], 0),
        )
    return values


def sum_rows(values):
    size = lax.axis_size("frames")
    bits = []
    bit = 1
    while bit < size:
        bits.append(bit)
        bit *= 2
    unit = 8 * size
    rows = values.shape[0]
    padded = -(-rows // unit) * unit
    values = jnp.pad(values, ((0, padded - rows), (0, 0)))
    cut = (padded // unit + 1) // 2 * unit
    first = sum_over_frames(values[:cut], bits)
    second = sum_over_frames(values[cut:], [bits[1], bits[0]] + bits[2:])
    return jnp.concatenate([first, second], 0)[:rows]


def sample_groups():
    groups = []
    for block in range(lax.axis_size("frames") // CLIP):
        for half in range(2):
            groups.append(
                [
                    2 * (block * CLIP + half * HALF + place) + core
                    for core in range(2)
                    for place in range(HALF)
                ]
            )
    return groups


def swap_samples(values):
    size = lax.axis_size("frames")
    pairs = []
    for frame in range(size):
        half = (frame % CLIP) // HALF
        pairs.append((2 * frame + 1 - half, 2 * (frame ^ HALF) + half))
    return lax.ppermute(values, ("frames", "dp"), pairs)


def shards(
    latents,
    noise,
    timesteps,
    image_flags,
    frame_counts,
    text,
    conv_in,
    res_convs,
    conv_out,
    time_w1,
    time_w2,
    temb_w,
    spatial_squares,
    cross_kv,
    spatial_up,
    spatial_down,
    frozen_vectors,
    motion_squares,
    motion_up,
    motion_down,
    motion_vectors,
    square_moment,
    up_moment,
    down_moment,
    vector_moment1,
    vector_moment2,
    square_ema,
    up_ema,
    down_ema,
    vector_ema,
):
    dp_index = lax.axis_index("dp")
    place = lax.axis_index("frames")
    block = place // CLIP
    place = place % CLIP
    half = place // HALF
    stays = half == dp_index
    frame = jnp.where(stays, place, (place + HALF) % CLIP)
    frozen_prepared = prepare_spatial(spatial_squares)
    pair = jnp.concatenate([latents.reshape(PIX, CHAN).T, noise.reshape(PIX, CHAN).T], axis=0)
    pair = jnp.where(stays, pair, swap_samples(pair)).astype(F32)

    def of_block(values):
        return lax.dynamic_index_in_dim(values[0], block, 0, keepdims=False)

    step_count = of_block(timesteps)
    facts = jnp.stack([step_count // 32, step_count % 32, of_block(image_flags)])
    facts = jnp.pad(facts.astype(BF16)[None, :], ((0, 0), (0, TEXT_DIM - 3)))
    text_facts = jnp.concatenate([of_block(text), facts], axis=0)
    text_facts = jnp.where(stays, text_facts, swap_cores(text_facts))
    facts = text_facts[TEXT_LEN].astype(F32)
    step_values = (facts[0] * 32.0 + facts[1])[None]
    flag = facts[2]
    phases = (step_values / 1000.0 + 0.008) / 1.008 * (math.pi / 2)
    keep_rate = jnp.cos(phases)[:, None]
    noise_rate = jnp.sin(phases)[:, None]
    spare = ((0, 8 - CHAN), (0, 0))
    noisy = jnp.pad(keep_rate * pair[:CHAN] + noise_rate * pair[CHAN:], spare)
    target = jnp.pad(keep_rate * pair[CHAN:] - noise_rate * pair[:CHAN], spare)
    temb_res = time_embed(step_values, time_w1, time_w2, temb_w, frozen_vectors[22])
    w_in = jnp.pad(conv_in.reshape(TAPS, CHAN, WIDTH), ((0, 0), (0, 8 - CHAN), (0, 0)))
    w_head = jnp.swapaxes(conv_out.reshape(TAPS, WIDTH, CHAN), 1, 2)
    w_head = jnp.pad(w_head, ((0, 0), (0, 8 - CHAN), (0, 0))).reshape(8 * TAPS, WIDTH)
    resnet, tokens = resnet_block(
        noisy,
        frozen_vectors,
        temb_res,
        w_in.reshape(8 * TAPS, WIDTH),
        res_convs.reshape(2, 3, 3 * WIDTH, WIDTH),
        spatial_squares[0],
    )
    hidden, packed = transformer_block(
        tokens, resnet, text_facts, frozen_vectors, frozen_prepared, cross_kv, spatial_up, spatial_down,
        spatial_squares[7],
    )
    groups = sample_groups()

    def exchange(values):
        return lax.all_to_all(
            values, ("frames", "dp"), split_axis=0, concat_axis=0, tiled=True, axis_index_groups=groups
        )

    arrived = exchange(packed)
    count = lax.dynamic_slice(frame_counts, (half, block), (1, 1)).reshape(1)
    keep = jnp.reshape(1.0 - flag, (1,))
    weights = prepare(motion_squares, motion_up, motion_down)
    branch, u, u2, u3, qkv1, qkv2, o1, o2, last = motion_forward(
        arrived, count, keep, weights, motion_vectors
    )
    frame_valid = (frame < count[0]).astype(F32)
    total_count = 4.0 * PIX * jnp.sum(frame_counts).astype(F32)
    grad, loss_part = head_block(
        frame_valid.reshape(1), total_count.reshape(1), hidden, exchange(branch), target, frozen_vectors, w_head
    )
    grad_in = exchange(grad)
    du3, early, g9, feed_sums = feed_backward(grad_in, keep, weights, motion_vectors, u3, last)
    du2, g5, g6, g7, g8, second_sums = second_backward(
        du3, count, weights, motion_vectors, u2, qkv2, o2
    )
    late = first_backward(
        du2, count, loss_part[0], arrived, weights, motion_vectors, u, qkv1, o1,
        (g5, g6, g7, g8, g9, feed_sums, second_sums),
    )
    core = dp_index.reshape(1)

    def sum_over_devices(both):
        own = lax.dynamic_index_in_dim(both, dp_index, 0, keepdims=False)
        other = lax.dynamic_index_in_dim(both, 1 - dp_index, 0, keepdims=False)
        return sum_rows(own + swap_cores(other))

    early = sum_over_devices(early)
    up_moment_new, down_moment_new, ahead = wide_moments(early, up_moment, down_moment)
    sent = lax.dynamic_slice_in_dim(ahead, (1 - dp_index) * DOWN_TILES, UP_TILES, 0)
    wide = wide_direction(core, ahead, swap_cores(sent))
    up_new, up_ema_new, down_new, down_ema_new = wide_update(
        core, wide, swap_cores(wide), motion_up, motion_down, up_ema, down_ema
    )
    late = sum_over_devices(late)
    square, square_moment_new, moment_first, moment_second, vector_new, vector_ema_new, loss_row = square_directions(
        late, square_moment, vector_moment1, vector_moment2, motion_vectors, vector_ema
    )
    square_new, square_ema_new = square_update(
        core, square, swap_cores(square), motion_squares, square_ema
    )
    return (
        loss_row[0, 0],
        total_count,
        square_new,
        square_moment_new,
        square_ema_new,
        up_new,
        up_moment_new,
        up_ema_new,
        down_new,
        down_moment_new,
        down_ema_new,
        moment_first,
        moment_second,
        vector_new,
        vector_ema_new,
    )


def solution(mesh):
    return jax.shard_map(
        shards,
        mesh=mesh,
        in_specs=(
            P("dp", "frames", None, None),
            P("dp", "frames", None, None),
            P("dp", None),
            P("dp", None),
            P(),
            P("dp", None, None, None),
            P(),
            P(),
            P(),
            P(),
            P(),
            P(),
            P(),
            P(),
            P(),
            P(),
            P(),
            P(),
            P(),
            P(),
            P(),
            P("dp", None, None),
            P(None, "dp"),
            P("dp", None),
            P(),
            P(),
            P("dp", None, None),
            P(None, "dp"),
            P("dp", None),
            P(),
        ),
        out_specs=(
            P(),
            P(),
            P(),
            P("dp", None, None),
            P("dp", None, None),
            P(),
            P(None, "dp"),
            P(None, "dp"),
            P(),
            P("dp", None),
            P("dp", None),
            P(),
            P(),
            P(),
            P(),
        ),
        check_vma=False,
    )
```

time: 1260 us -> 483 us (0.38)
  waiting for transfers between devices: 499 us -> 97.2 us
  Pallas kernels: 0 us -> 263 us
  matrix products: 257 us -> 3.53 us
  local copies, waits for them, and re-layouts: 167 us -> 34.5 us
  loops' own time: 123 us -> 0 us
  blocking collectives: 80.1 us -> 0 us
  other arithmetic: 87.7 us -> 13.8 us
  starting transfers between devices: 18.3 us -> 56.6 us
  between operations: 20.4 us -> 7.58 us
    psum x2 -> x0, waiting for transfers between devices: 442 us -> none  [the longest x1 247 us: shards(): lax.psum((jnp.stack(results[:10]), results[10], results[11]), 'frames')]
    pallas_call x0 -> x14, Pallas kernels: none -> 263 us  [the longest x1 41.2 us: transformer_block(): pl.pallas_call(transformer_kernel, in_specs=[in_vmem()] * len(operands),...]
    dot_general x51 -> x0, matrix products: 124 us -> none  [the longest x12 36.7 us: product_back(): jnp.einsum('...j,ij->...i', left, right, preferred_element_type=jnp.float32)]
    another operation x12 -> x0, loops' own time: 123 us -> none  [shards(): lax.cond(frame_index == owner_id, orthogonalize, jnp.zeros_like, matrix)]
    ppermute x0 -> x39, waiting for transfers between devices: none -> 82.7 us  [the longest x32 82.4 us: swap_frames(): return lax.ppermute(values, 'frames', [(i, i ^ bit) for i in range(size)])]
    psum x1 -> x0, blocking collectives: 80.1 us -> none  [shards(): lax.psum(jnp.sum(frame_valid * jnp.square(residual)), ('frames', 'dp'))]
    convert_element_type x38 -> x2, local copies, waits for them, and re-layouts: 64 us -> 0.01 us  [to_low(): return values.astype(BF16)]
    dot_general x25 -> x3, matrix products: 62.9 us -> 3.53 us  [product(): jnp.einsum('...i,ij->...j', left, right, preferred_element_type=jnp.float32)]
  transfers between devices with their start and end apart: 8 -> 42, of which waited for: 8 -> 20; matrix products, arithmetic and copies ran while one was open for 2% -> 7% of each run, Pallas kernels for 0% -> 13%
where the time goes in v2:
time: 483 us; the launch traced here: 476 us
  Pallas kernels  263 us (54%)
  waiting for transfers between devices  97.2 us (20%)
  starting transfers between devices  56.6 us (12%)
  local copies, waits for them, and re-layouts  34.5 us (7%)
  other arithmetic  13.8 us (3%)
  between operations  7.58 us (2%)
    ppermute x32, waiting for transfers between devices, swap_frames(): return lax.ppermute(values, 'frames', [(i, i ^ bit) for i in range(size)])  82.4 us
    pallas_call x1, Pallas kernels, transformer_block(): pl.pallas_call(transformer_kernel, in_specs=[in_vmem()] * len(operands),...  41.2 us
    pallas_call x1, Pallas kernels, square_directions(): pl.pallas_call(square_directions_kernel, in_specs=[in_vmem()] * 6, out_sp...  36.1 us
    ppermute x32, starting transfers between devices, swap_frames(): return lax.ppermute(values, 'frames', [(i, i ^ bit) for i in range(size)])  34.8 us
    pallas_call x1, Pallas kernels, first_backward(): pl.pallas_call(first_backward_kernel, grid=(CHUNKS,), in_specs=[in_smem()...  31.1 us
    pallas_call x1, Pallas kernels, motion_forward(): pl.pallas_call(motion_forward_kernel, grid=(CHUNKS,), in_specs=[in_smem()...  29.4 us
    pallas_call x1, Pallas kernels, second_backward(): pl.pallas_call(second_backward_kernel, grid=(CHUNKS,), in_specs=[in_smem(...  25.4 us
    pallas_call x1, Pallas kernels, feed_backward(): pl.pallas_call(feed_backward_kernel, grid=(CHUNKS,), in_specs=[in_smem()]...  22.8 us
  transfers between devices with their start and end apart: 42, of which 20 were waited for; matrix products, arithmetic and copies ran while one was open for 7% of the time, Pallas kernels for 13%

profile of v2, /device:TPU:0, one launch (start us, length us, event | category | flops | bytes accessed | tf_op | source)
XLA Modules:
  0.0 476.1 jit_solution(16840878886764270310)
XLA Ops:
  5.8 4.9 %collective-permute-start = (bf16[78,768]{1,0:T(8,128)(2,1)S(1)}, bf16[78,768]{1,0:T(8,128)(2,1)}, u32[]{:S(2)}, u32[]{:S(2)}) collective-permute-start(bf16[78,768]{1,0:T(8,128)(2,1)S(1)} %pad_maximum_fusion.2), channel_id=1, source_target_pairs={{0,1},{1,0},{2,3},{3,2},{4,5},{5,4},{6,7},{7,6},{8,9},{9,8},{10,11... | collective-permute-start | bytes 359432 | tf_op jit(solution)/shard_map/ppermute | solution.py:1116
  27.9 17.7 %resnet_block.1 = (f32[1024,320]{1,0:T(8,128)}, f32[1024,320]{1,0:T(8,128)}) custom-call(f32[8,1024]{1,0:T(8,128)} %pad.19.noisy_ref, f32[23,320]{1,0:T(8,128)} %vec_ref.11, f32[1,320]{1,0:T(1,128)} %convolution_add_fusion.temb_ref, bf16[320,320]{1,0:T(8,128)(2,1)} %constant.333.clone.ones_ref, bf16[72,320]{1,0:T(8,128)(2,1)} %pad_bitcast_fusion.1.w_in_ref, ...), custom_call_target="tpu_custom_call" | custom-call | tf_op jit(solution)/shard_map/resnet_block/pallas_call | solution.py:882
  45.6 41.2 %transformer_block.1 = (f32[1024,320]{1,0:T(8,128)}, bf16[16,160,128]{2,1,0:T(8,128)(2,1)}) custom-call(f32[1024,320]{1,0:T(8,128)} %get-tuple-element.72.tokens_ref, f32[1024,320]{1,0:T(8,128)} %get-tuple-element.73.resnet_ref, bf16[78,768]{1,0:T(8,128)(2,1)} %copy-done.12, f32[23,320]{1,0:T(8,128)} %vec_ref.11, bf16[320,320]{1,0:T(8,128)(2,1)} %constant.333.clone.ones_ref, ...), custom_call_target="tpu_custom_call" | custom-call | tf_op jit(solution)/shard_map/transformer_block/pallas_call | solution.py:1014
  86.8 5.1 %all-to-all-start = ((bf16[16,160,128]{2,1,0:T(8,128)(2,1)}), bf16[16,160,128]{2,1,0:T(8,128)(2,1)S(1)}, u32[]{:S(2)}, u32[]{:S(2)}) async-start(bf16[16,160,128]{2,1,0:T(8,128)(2,1)} %get-tuple-element.79), calls=%async_computation | async-start | bytes 1310720 | tf_op jit(solution)/shard_map/all_to_all | solution.py:1264
  94.3 9.8 %motion_weights.1 = (bf16[320,320]{1,0:T(8,128)(2,1)}, bf16[2,320,1536]{2,1,0:T(8,128)(2,1)}, bf16[2,512,320]{2,1,0:T(8,128)(2,1)}, bf16[320,2560]{1,0:T(8,128)(...) custom-call(f32[10,320,320]{2,1,0:T(8,128)} %weight_ref.1, ...), custom_call_target="tpu_custom_call" | custom-call | tf_op jit(solution)/shard_map/motion_weights/pallas_call | solution.py:275
  105.6 29.4 %motion_forward.1 = (bf16[16,160,128]{2,1,0:T(8,128)(2,1)}, f32[1024,320]{1,0:T(8,128)}, f32[1024,320]{1,0:T(8,128)}, f32[1024,320]{1,0:T(8,128)}, bf16[1024,153...) custom-call(s32[1]{0:T(128)} %bitcast.count_ref, ...), custom_call_target="tpu_custom_call" | custom-call | tf_op jit(solution)/shard_map/motion_forward/pallas_call | solution.py:233
  135.0 5.2 %all-to-all-start.1 = ((bf16[16,160,128]{2,1,0:T(8,128)(2,1)}), bf16[16,160,128]{2,1,0:T(8,128)(2,1)S(1)}, u32[]{:S(2)}, u32[]{:S(2)}) async-start(bf16[16,160,128]{2,1,0:T(8,128)(2,1)} %get-tuple-element.86), calls=%async_computation.1 | async-start | bytes 1310720 | tf_op jit(solution)/shard_map/all_to_all | solution.py:1264
  143.4 7.5 %all-to-all-done.1.branch_ref = bf16[16,160,128]{2,1,0:T(8,128)(2,1)S(1)} async-done(((bf16[16,160,128]{2,1,0:T(8,128)(2,1)}), bf16[16,160,128]{2,1,0:T(8,128)(2,1)S(1)}, u32[]{:S(2)}, u32[]{:S(2)}) %all-to-all-start.1) | async-done | bytes 655392 | tf_op jit(solution)/shard_map/all_to_all | solution.py:1264
  151.8 6.0 %head_block.1 = (bf16[16,160,128]{2,1,0:T(8,128)(2,1)}, f32[1,1]{1,0:T(1,128)}) custom-call(f32[1]{0:T(128)} %bitcast.2.valid_ref, f32[1]{0:T(128)} %bitcast.3.total_ref, f32[1024,320]{1,0:T(8,128)} %get-tuple-element.78.hidden_ref, bf16[16,160,128]{2,1,0:T(8,128)(2,1)} %copy-done.4, f32[8,1024]{1,0:T(8,128)} %pad.21.target_ref, f32[23,320]{1,0:T(8,128)} %vec_ref.11, ...), custom_call_target="tpu_custom_call" | custom-call | tf_op jit(solution)/shard_map/head_block/pallas_call | solution.py:1086
  165.5 7.1 %all-to-all-done.2.grad_ref = bf16[16,160,128]{2,1,0:T(8,128)(2,1)S(1)} async-done(((bf16[16,160,128]{2,1,0:T(8,128)(2,1)}), bf16[16,160,128]{2,1,0:T(8,128)(2,1)S(1)}, u32[]{:S(2)}, u32[]{:S(2)}) %all-to-all-start.2) | async-done | bytes 655392 | tf_op jit(solution)/shard_map/all_to_all | solution.py:1264
  173.4 22.8 %feed_backward.1 = (f32[1024,320]{1,0:T(8,128)}, f32[2,4864,128]{2,1,0:T(8,128)}, f32[320,320]{1,0:T(8,128)}, f32[8,320]{1,0:T(8,128)}) custom-call(f32[1]{0:T(128)} %bitcast.18.keep_ref, bf16[16,160,128]{2,1,0:T(8,128)(2,1)} %copy-done.3, f32[1024,320]{1,0:T(8,128)} %get-tuple-element.89.u3_ref, bf16[1024,320]{1,0:T(8,128)(2,1)} %get-tuple-element.90.last_ref, ...), custom_call_target="tpu_custom_call" | custom-call | tf_op jit(solution)/shard_map/feed_backward/pallas_call | solution.py:346
  196.2 25.4 %second_backward.1 = (f32[1024,320]{1,0:T(8,128)}, f32[320,320]{1,0:T(8,128)}, f32[320,320]{1,0:T(8,128)}, f32[320,320]{1,0:T(8,128)}, f32[320,320]{1,0:T(8,128)}, /*index=5*/f32[8,320]{1,0:T(8,128)}) custom-call(s32[1]{0:T(128)} %bitcast.count_ref, f32[1024,320]{1,0:T(8,128)} %get-tuple-element.94.grad_ref, f32[1024,320]{1,0:T(8,128)} %get-tuple-element.95.u2_ref, ...), custom_call_target="tpu_custom_call" | custom-call | tf_op jit(solution)/shard_map/second_backward/pallas_call | solution.py:428
  221.5 31.1 %first_backward.1 = f32[2,4224,128]{2,1,0:T(8,128)} custom-call(s32[1]{0:T(128)} %bitcast.count_ref, f32[1]{0:T(128)} %bitcast.22.loss_ref, f32[1024,320]{1,0:T(8,128)} %get-tuple-element.100.grad_ref, f32[1024,320]{1,0:T(8,128)} %get-tuple-element.101.u_ref, bf16[1024,1536]{1,0:T(8,128)(2,1)} %get-tuple-element.102.qkv_ref, ...), custom_call_target="tpu_custom_call" | custom-call | tf_op jit(solution)/shard_map/first_backward/pallas_call | solution.py:489
  269.7 7.5 %collective-permute-done.11 = f32[1024,128]{1,0:T(8,128)S(1)} collective-permute-done((f32[1024,128]{1,0:T(8,128)S(1)}, f32[1024,128]{1,0:T(8,128)S(1)}, u32[]{:S(2)}, u32[]{:S(2)}) %collective-permute-start.11) | collective-permute-done | bytes 524320 | tf_op jit(solution)/shard_map/ppermute | solution.py:1125
  280.3 17.3 %collective-permute-done.12 = f32[512,128]{1,0:T(8,128)S(1)} collective-permute-done((f32[512,128]{1,0:T(8,128)S(1)}, f32[512,128]{1,0:T(8,128)S(1)}, u32[]{:S(2)}, u32[]{:S(2)}) %collective-permute-start.12) | collective-permute-done | bytes 262176 | tf_op jit(solution)/shard_map/ppermute | solution.py:1125
  328.2 4.8 %collective-permute-done.33 = f32[152,128]{1,0:T(8,128)S(1)} collective-permute-done((f32[152,128]{1,0:T(8,128)S(1)}, f32[152,128]{1,0:T(8,128)S(1)}, u32[]{:S(2)}, u32[]{:S(2)}) %collective-permute-start.33) | collective-permute-done | bytes 77856 | tf_op jit(solution)/shard_map/ppermute | solution.py:1125
  342.0 6.8 %collective-permute-done.35 = f32[608,128]{1,0:T(8,128)S(1)} collective-permute-done((f32[608,128]{1,0:T(8,128)S(1)}, f32[608,128]{1,0:T(8,128)S(1)}, u32[]{:S(2)}, u32[]{:S(2)}) %collective-permute-start.35) | collective-permute-done | bytes 311328 | tf_op jit(solution)/shard_map/ppermute | solution.py:1125
  361.1 5.4 %wide_moments.1 = (f32[320,1280]{1,0:T(8,128)}, f32[640,320]{1,0:T(8,128)}, f32[15,320,128]{2,1,0:T(8,128)}) custom-call(f32[4864,128]{1,0:T(8,128)} %pad_maximum_fusion.sum_ref, f32[320,1280]{1,0:T(8,128)} %up_ref.4, f32[640,320]{1,0:T(8,128)} %copy.58.down_ref), custom_call_target="tpu_custom_call" | custom-call | tf_op jit(solution)/shard_map/wide_moments/pallas_call | solution.py:553
  370.3 6.6 %collective-permute-done.17 = f32[512,128]{1,0:T(8,128)S(1)} collective-permute-done((f32[512,128]{1,0:T(8,128)S(1)}, f32[512,128]{1,0:T(8,128)S(1)}, u32[]{:S(2)}, u32[]{:S(2)}) %collective-permute-start.17) | collective-permute-done | bytes 262176 | tf_op jit(solution)/shard_map/ppermute | solution.py:1125
  379.4 11.3 %collective-permute-done.18 = f32[1024,128]{1,0:T(8,128)S(1)} collective-permute-done((f32[1024,128]{1,0:T(8,128)S(1)}, f32[1024,128]{1,0:T(8,128)S(1)}, u32[]{:S(2)}, u32[]{:S(2)}) %collective-permute-start.18) | collective-permute-done | bytes 524320 | tf_op jit(solution)/shard_map/ppermute | solution.py:1125
  393.2 16.4 %wide_direction.1.own_ref = bf16[20,320,128]{2,1,0:T(8,128)(2,1)} custom-call(s32[1]{0:T(128)} %bitcast.30.core_ref, f32[15,320,128]{2,1,0:T(8,128)} %get-tuple-element.118.own_ref, f32[10,320,128]{2,1,0:T(8,128)} %collective-permute-done.37.got_ref), custom_call_target="tpu_custom_call" | custom-call | tf_op jit(solution)/shard_map/wide_direction/pallas_call | solution.py:606
  411.1 36.1 %square_directions.1 = (bf16[5,320,320]{2,1,0:T(8,128)(2,1)}, f32[5,320,320]{2,1,0:T(8,128)}, f32[13,320]{1,0:T(8,128)}, f32[13,320]{1,0:T(8,128)}, f32[13,320]{...) custom-call(f32[4224,128]{1,0:T(8,128)} %pad_maximum_fusion.1.sum_ref, f32[5,320,320]{2,1,0:T(8,128)} %moment_ref.1, ...), custom_call_target="tpu_custom_call" | custom-call | tf_op jit(solution)/shard_map/square_directions/pallas_call | solution.py:700
  451.5 8.6 %square_update.1 = (f32[10,320,320]{2,1,0:T(8,128)}, f32[5,320,320]{2,1,0:T(8,128)}) custom-call(s32[1]{0:T(128)} %bitcast.30.core_ref, bf16[5,320,320]{2,1,0:T(8,128)(2,1)} %get-tuple-element.113.own_ref, bf16[5,320,320]{2,1,0:T(8,128)(2,1)} %copy-done.7, f32[10,320,320]{2,1,0:T(8,128)} %weight_ref.1, f32[5,320,320]{2,1,0:T(8,128)} %ema_ref.1), custom_call_target="tpu_custom_call" | custom-call | tf_op jit(solution)/shard_map/square_update/pallas_call | solution.py:730
  460.1 9.1 %wide_update.1 = (f32[320,2560]{1,0:T(8,128)}, f32[320,1280]{1,0:T(8,128)}, f32[1280,320]{1,0:T(8,128)}, f32[640,320]{1,0:T(8,128)}) custom-call(s32[1]{0:T(128)} %bitcast.30.core_ref, bf16[20,320,128]{2,1,0:T(8,128)(2,1)} %wide_direction.1.own_ref, bf16[20,320,128]{2,1,0:T(8,128)(2,1)} %collective-permute-done.38.got_ref, f32[320,2560]{1,0:T(8,128)} %up_ref.5, ...), custom_call_target="tpu_custom_call" | custom-call | tf_op jit(solution)/shard_map/wide_update/pallas_call | solution.py:647
  (200 shorter events, 125.3 us)
Async XLA Ops:
  1.5 18.4 %collective-permute-start.1 = (bf16[8,1024]{1,0:T(8,128)(2,1)S(1)}, bf16[8,1024]{1,0:T(8,128)(2,1)}, u32[]{:S(2)}, u32[]{:S(2)}) collective-permute-start(bf16[8,1024]{1,0:T(8,128)(2,1)S(1)} %pad_maximum_fusion.3), channel_id=1, source_target_pairs={{1,16},{3,18},{5,20},{7,22},{9,24},{11,26},{13,28},{15,30},{16,1},... | collective-permute-start | bytes 49160 | tf_op jit(solution)/shard_map/ppermute | solution.py:1182
  5.8 14.8 %collective-permute-start = (bf16[78,768]{1,0:T(8,128)(2,1)S(1)}, bf16[78,768]{1,0:T(8,128)(2,1)}, u32[]{:S(2)}, u32[]{:S(2)}) collective-permute-start(bf16[78,768]{1,0:T(8,128)(2,1)S(1)} %pad_maximum_fusion.2), channel_id=1, source_target_pairs={{0,1},{1,0},{2,3},{3,2},{4,5},{5,4},{6,7},{7,6},{8,9},{9,8},{10,11... | collective-permute-start | bytes 359432 | tf_op jit(solution)/shard_map/ppermute | solution.py:1116
  86.8 17.9 %all-to-all-start = ((bf16[16,160,128]{2,1,0:T(8,128)(2,1)}), bf16[16,160,128]{2,1,0:T(8,128)(2,1)S(1)}, u32[]{:S(2)}, u32[]{:S(2)}) async-start(bf16[16,160,128]{2,1,0:T(8,128)(2,1)} %get-tuple-element.79), calls=%async_computation | async-start | bytes 1310720 | tf_op jit(solution)/shard_map/all_to_all | solution.py:1264
  135.0 15.9 %all-to-all-start.1 = ((bf16[16,160,128]{2,1,0:T(8,128)(2,1)}), bf16[16,160,128]{2,1,0:T(8,128)(2,1)S(1)}, u32[]{:S(2)}, u32[]{:S(2)}) async-start(bf16[16,160,128]{2,1,0:T(8,128)(2,1)} %get-tuple-element.86), calls=%async_computation.1 | async-start | bytes 1310720 | tf_op jit(solution)/shard_map/all_to_all | solution.py:1264
  157.8 14.7 %all-to-all-start.2 = ((bf16[16,160,128]{2,1,0:T(8,128)(2,1)}), bf16[16,160,128]{2,1,0:T(8,128)(2,1)S(1)}, u32[]{:S(2)}, u32[]{:S(2)}) async-start(bf16[16,160,128]{2,1,0:T(8,128)(2,1)} %get-tuple-element.88), calls=%async_computation.2 | async-start | bytes 1310720 | tf_op jit(solution)/shard_map/all_to_all | solution.py:1264
  262.4 14.8 %collective-permute-start.11 = (f32[1024,128]{1,0:T(8,128)S(1)}, f32[1024,128]{1,0:T(8,128)S(1)}, u32[]{:S(2)}, u32[]{:S(2)}) collective-permute-start(f32[1024,128]{1,0:T(8,128)S(1)} %constant_dynamic-slice_fusion.12), channel_id=1, source_target_pairs={{0,4},{2,6},{4,0},{6,2},{8,12},{10,14},{12,8},{14,10},{16,20},{18,... | collective-permute-start | bytes 1572872 | tf_op jit(solution)/shard_map/ppermute | solution.py:1125
  264.3 15.6 %collective-permute-start.3 = (f32[1088,128]{1,0:T(8,128)S(1)}, f32[1088,128]{1,0:T(8,128)S(1)}, u32[]{:S(2)}, u32[]{:S(2)}) collective-permute-start(f32[1088,128]{1,0:T(8,128)S(1)} %constant_dynamic-slice_fusion.16), channel_id=1, source_target_pairs={{0,2},{2,0},{4,6},{6,4},{8,10},{10,8},{12,14},{14,12},{16,18},{18,... | collective-permute-start | bytes 1671176 | tf_op jit(solution)/shard_map/ppermute | solution.py:1125
  267.9 35.9 %collective-permute-start.29 = (f32[1216,128]{1,0:T(8,128)S(1)}, f32[1216,128]{1,0:T(8,128)S(1)}, u32[]{:S(2)}, u32[]{:S(2)}) collective-permute-start(f32[1216,128]{1,0:T(8,128)S(1)} %constant_dynamic-slice_fusion.4), channel_id=1, source_target_pairs={{0,4},{2,6},{4,0},{6,2},{8,12},{10,14},{12,8},{14,10},{16,20},{18,... | collective-permute-start | bytes 1867784 | tf_op jit(solution)/shard_map/ppermute | solution.py:1125
  269.0 35.5 %collective-permute-start.21 = (f32[1216,128]{1,0:T(8,128)S(1)}, f32[1216,128]{1,0:T(8,128)S(1)}, u32[]{:S(2)}, u32[]{:S(2)}) collective-permute-start(f32[1216,128]{1,0:T(8,128)S(1)} %constant_dynamic-slice_fusion.8), channel_id=1, source_target_pairs={{0,2},{2,0},{4,6},{6,4},{8,10},{10,8},{12,14},{14,12},{16,18},{18,... | collective-permute-start | bytes 1867784 | tf_op jit(solution)/shard_map/ppermute | solution.py:1125
  277.3 20.3 %collective-permute-start.12 = (f32[512,128]{1,0:T(8,128)S(1)}, f32[512,128]{1,0:T(8,128)S(1)}, u32[]{:S(2)}, u32[]{:S(2)}) collective-permute-start(f32[512,128]{1,0:T(8,128)S(1)} %constant_dynamic-slice_fusion.11), channel_id=1, source_target_pairs={{0,2},{2,0},{4,6},{6,4},{8,10},{10,8},{12,14},{14,12},{16,18},{18,... | collective-permute-start | bytes 786440 | tf_op jit(solution)/shard_map/ppermute | solution.py:1125
  280.0 18.4 %collective-permute-start.4 = (f32[544,128]{1,0:T(8,128)S(1)}, f32[544,128]{1,0:T(8,128)S(1)}, u32[]{:S(2)}, u32[]{:S(2)}) collective-permute-start(f32[544,128]{1,0:T(8,128)S(1)} %constant_dynamic-slice_fusion.15), channel_id=1, source_target_pairs={{0,4},{2,6},{4,0},{6,2},{8,12},{10,14},{12,8},{14,10},{16,20},{18,... | collective-permute-start | bytes 835592 | tf_op jit(solution)/shard_map/ppermute | solution.py:1125
  303.5 37.4 %collective-permute-start.14 = (f32[128,128]{1,0:T(8,128)S(1)}, f32[128,128]{1,0:T(8,128)S(1)}, u32[]{:S(2)}, u32[]{:S(2)}) collective-permute-start(f32[128,128]{1,0:T(8,128)S(1)} %constant_dynamic-slice_fusion.9), channel_id=1, source_target_pairs={{0,16},{2,18},{4,20},{6,22},{8,24},{10,26},{12,28},{14,30},{16,0},... | collective-permute-start | bytes 196616 | tf_op jit(solution)/shard_map/ppermute | solution.py:1125
  335.3 15.1 %collective-permute-start.6 = (f32[136,128]{1,0:T(8,128)S(1)}, f32[136,128]{1,0:T(8,128)S(1)}, u32[]{:S(2)}, u32[]{:S(2)}) collective-permute-start(f32[136,128]{1,0:T(8,128)S(1)} %constant_dynamic-slice_fusion.13), channel_id=1, source_target_pairs={{0,16},{2,18},{4,20},{6,22},{8,24},{10,26},{12,28},{14,30},{16,0},... | collective-permute-start | bytes 208904 | tf_op jit(solution)/shard_map/ppermute | solution.py:1125
  338.4 10.4 %collective-permute-start.35 = (f32[608,128]{1,0:T(8,128)S(1)}, f32[608,128]{1,0:T(8,128)S(1)}, u32[]{:S(2)}, u32[]{:S(2)}) collective-permute-start(f32[608,128]{1,0:T(8,128)S(1)} %maximum_select_fusion.9), channel_id=1, source_target_pairs={{0,2},{2,0},{4,6},{6,4},{8,10},{10,8},{12,14},{14,12},{16,18},{18,... | collective-permute-start | bytes 933896 | tf_op jit(solution)/shard_map/ppermute | solution.py:1125
  341.0 10.7 %collective-permute-start.15 = (f32[128,128]{1,0:T(8,128)S(1)}, f32[128,128]{1,0:T(8,128)S(1)}, u32[]{:S(2)}, u32[]{:S(2)}) collective-permute-start(f32[128,128]{1,0:T(8,128)S(1)} %dynamic-slice_add_fusion.15), channel_id=1, source_target_pairs={{0,16},{2,18},{4,20},{6,22},{8,24},{10,26},{12,28},{14,30},{16,0},... | collective-permute-start | bytes 196616 | tf_op jit(solution)/shard_map/ppermute | solution.py:1125
  348.8 10.3 %collective-permute-start.36 = (f32[1216,128]{1,0:T(8,128)S(1)}, f32[1216,128]{1,0:T(8,128)S(1)}, u32[]{:S(2)}, u32[]{:S(2)}) collective-permute-start(f32[1216,128]{1,0:T(8,128)S(1)} %maximum_select_fusion.5), channel_id=1, source_target_pairs={{0,4},{2,6},{4,0},{6,2},{8,12},{10,14},{12,8},{14,10},{16,20},{18,... | collective-permute-start | bytes 1867784 | tf_op jit(solution)/shard_map/ppermute | solution.py:1125
  349.0 10.3 %collective-permute-start.28 = (f32[1216,128]{1,0:T(8,128)S(1)}, f32[1216,128]{1,0:T(8,128)S(1)}, u32[]{:S(2)}, u32[]{:S(2)}) collective-permute-start(f32[1216,128]{1,0:T(8,128)S(1)} %maximum_select_fusion.4), channel_id=1, source_target_pairs={{0,2},{2,0},{4,6},{6,4},{8,10},{10,8},{12,14},{14,12},{16,18},{18,... | collective-permute-start | bytes 1867784 | tf_op jit(solution)/shard_map/ppermute | solution.py:1125
  351.7 16.4 %collective-permute-start.16 = (f32[256,128]{1,0:T(8,128)S(1)}, f32[256,128]{1,0:T(8,128)S(1)}, u32[]{:S(2)}, u32[]{:S(2)}) collective-permute-start(f32[256,128]{1,0:T(8,128)S(1)} %maximum_select_fusion.15), channel_id=1, source_target_pairs={{0,8},{2,10},{4,12},{6,14},{8,0},{10,2},{12,4},{14,6},{16,24},{18,... | collective-permute-start | bytes 393224 | tf_op jit(solution)/shard_map/ppermute | solution.py:1125
  356.3 13.2 %collective-permute-start.8 = (f32[272,128]{1,0:T(8,128)S(1)}, f32[272,128]{1,0:T(8,128)S(1)}, u32[]{:S(2)}, u32[]{:S(2)}) collective-permute-start(f32[272,128]{1,0:T(8,128)S(1)} %maximum_select_fusion.14), channel_id=1, source_target_pairs={{0,8},{2,10},{4,12},{6,14},{8,0},{10,2},{12,4},{14,6},{16,24},{18,... | collective-permute-start | bytes 417800 | tf_op jit(solution)/shard_map/ppermute | solution.py:1125
  368.0 25.2 %collective-permute-start.37 = (f32[10,320,128]{2,1,0:T(8,128)S(1)}, f32[10,320,128]{2,1,0:T(8,128)}, u32[]{:S(2)}, u32[]{:S(2)}) collective-permute-start(f32[10,320,128]{2,1,0:T(8,128)S(1)} %constant_dynamic-slice_fusion), channel_id=1, source_target_pairs={{0,1},{1,0},{2,3},{3,2},{4,5},{5,4},{6,7},{7,6},{8,9},{9,8},{10,11... | collective-permute-start | bytes 4915208 | tf_op jit(solution)/shard_map/ppermute | solution.py:1116
  369.6 9.4 %collective-permute-start.9 = (f32[544,128]{1,0:T(8,128)S(1)}, f32[544,128]{1,0:T(8,128)S(1)}, u32[]{:S(2)}, u32[]{:S(2)}) collective-permute-start(f32[544,128]{1,0:T(8,128)S(1)} %maximum_select_fusion.10), channel_id=1, source_target_pairs={{0,4},{2,6},{4,0},{6,2},{8,12},{10,14},{12,8},{14,10},{16,20},{18,... | collective-permute-start | bytes 835592 | tf_op jit(solution)/shard_map/ppermute | solution.py:1125
  377.0 13.8 %collective-permute-start.18 = (f32[1024,128]{1,0:T(8,128)S(1)}, f32[1024,128]{1,0:T(8,128)S(1)}, u32[]{:S(2)}, u32[]{:S(2)}) collective-permute-start(f32[1024,128]{1,0:T(8,128)S(1)} %maximum_select_fusion.7), channel_id=1, source_target_pairs={{0,4},{2,6},{4,0},{6,2},{8,12},{10,14},{12,8},{14,10},{16,20},{18,... | collective-permute-start | bytes 1572872 | tf_op jit(solution)/shard_map/ppermute | solution.py:1125
  379.0 14.0 %collective-permute-start.10 = (f32[1088,128]{1,0:T(8,128)S(1)}, f32[1088,128]{1,0:T(8,128)S(1)}, u32[]{:S(2)}, u32[]{:S(2)}) collective-permute-start(f32[1088,128]{1,0:T(8,128)S(1)} %maximum_select_fusion.6), channel_id=1, source_target_pairs={{0,2},{2,0},{4,6},{6,4},{8,10},{10,8},{12,14},{14,12},{16,18},{18,... | collective-permute-start | bytes 1671176 | tf_op jit(solution)/shard_map/ppermute | solution.py:1125
  409.6 50.5 %collective-permute-start.38 = (bf16[20,320,128]{2,1,0:T(8,128)(2,1)}, bf16[20,320,128]{2,1,0:T(8,128)(2,1)}, u32[]{:S(2)}, u32[]{:S(2)}) collective-permute-start(bf16[20,320,128]{2,1,0:T(8,128)(2,1)} %wide_direction.1.own_ref), channel_id=1, source_target_pairs={{0,1},{1,0},{2,3},{3,2},{4,5},{5,4},{6,7},{7,6},{8,9},{9,8},{10,11... | collective-permute-start | bytes 4915208 | tf_op jit(solution)/shard_map/ppermute | solution.py:1116
  (35 other events, 301.1 us)
